TPU v7x, 32 devices: a whole 2x2x4 slice. The times are simulated.
32 devices in a mesh: groups: 2 (over y), tensor: 4 (over x, core), dp: 4 (over z).
Axes of the slice: x: 2, y: 2, z: 4, core: 2. Of those that a mesh axis runs over, the one named last changes fastest.
Arguments:
- hidden_input: bfloat16 [2048, 8192], P(('groups', 'dp'), 'tensor'), parts along dimension 0, may hold values from -6 to 6
- input_weight: bfloat16 [8192, 8192], P(None, 'tensor'), may hold values from -0.0625 to 0.0625
- kernel_weight: float32 [4, 8192], P(None, 'tensor'), may hold values from -3 to 3
- kernel_bias: float32 [8192], P('tensor'), may hold values from -3 to 3
- select_weight: bfloat16 [8192, 544], P('tensor'), may hold values from -0.0625 to 0.0625
- step_gain: float32 [512], replicated, may hold values from 0.1 to 1.9
- step_weight: bfloat16 [512, 8192], P(None, 'tensor'), may hold values from -0.25 to 0.25
- step_bias: float32 [8192], P('tensor'), may hold values from -6 to -2
- decay_log: float32 [16, 8192], P(None, 'tensor'), may hold values from 0 to 2.77
- skip_gain: float32 [8192], P('tensor'), may hold values from 0.5 to 1.5
- state_cache: bfloat16 [640, 16, 8192], P(('groups', 'dp'), None, 'tensor'), parts along dimension 0, may hold values from -3 to 3
- window_cache: bfloat16 [640, 3, 8192], P(('groups', 'dp'), None, 'tensor'), parts along dimension 0, may hold values from -6 to 6
- cache_owner: int32 [512], P(('groups', 'dp')), parts along dimension 0, may hold values from 0 to 3, as said below
- cache_slot: int32 [512], P(('groups', 'dp')), parts along dimension 0, may hold values from 0 to 79, as said below
- accepted: int32 [512], P(('groups', 'dp')), parts along dimension 0, may hold values from 0 to 4
Outputs:
- mamba_output: bfloat16 [2048, 8192], P(('groups', 'dp'), 'tensor'), parts along dimension 0
- new_state_cache: bfloat16 [640, 16, 8192], P(('groups', 'dp'), None, 'tensor'), parts along dimension 0
- new_window_cache: bfloat16 [640, 3, 8192], P(('groups', 'dp'), None, 'tensor'), parts along dimension 0
There are 2 independent parts, one for each index of `groups`. A program takes and returns all parts, laid end to end along the dimension named above; an argument that names none is the same for every part. Nothing has to cross between parts.
Inputs may be any that keep to these rules, and one draw needn't show every extreme that they name: `cache_owner`: at most 32 requests of one index of dp share an owner, and among the requests of every index of dp some owner has exactly 32; every owner holds exactly 64 requests. `cache_slot`: no two requests share both owner and slot.
All inputs are finite; a program needn't handle non-finite values.
Results may differ from a plain program's by a relative error of at most 0.0095.
Values may be sent and summed in bfloat16 or wider, within the bound.
A program may use at most 192 MiB of HBM per device.

v0:
```python
import jax
import jax.numpy as jnp
from jax import lax
from jax.sharding import PartitionSpec as P

epsilon = 1e-06


def project_input(hidden_input, input_weight):
    summed = jnp.dot(
        lax.all_gather(hidden_input, "tensor", axis=1, tiled=True),
        input_weight,
        preferred_element_type=jnp.float32,
    )
    return summed.astype(jnp.bfloat16)


def convolve(inputs, earlier_inputs, kernel_weight, kernel_bias):
    draft_steps = inputs.shape[1]
    window = jnp.concatenate([earlier_inputs, inputs], axis=1)
    mixed = kernel_bias + kernel_weight[0] * window[:, 0:draft_steps].astype(jnp.float32)
    for tap_index in range(1, kernel_weight.shape[0]):
        mixed = mixed + kernel_weight[tap_index] * window[
            :, tap_index : tap_index + draft_steps
        ].astype(jnp.float32)
    return (jax.nn.silu(mixed).astype(jnp.bfloat16), window)


def gates(activated_rows, select_weight, step_gain, step_weight, step_bias, states):
    partial_value = jnp.dot(activated_rows, select_weight, preferred_element_type=jnp.float32)
    projected = lax.psum(partial_value, "tensor")
    rank_width = step_gain.shape[0]
    rank_part = projected[:, :rank_width]
    norm_scale = lax.rsqrt(jnp.mean(rank_part * rank_part, axis=1, keepdims=True) + epsilon)
    rank_normed = (rank_part * norm_scale * step_gain).astype(jnp.bfloat16)
    step_size = jax.nn.softplus(
        jnp.dot(rank_normed, step_weight, preferred_element_type=jnp.float32) + step_bias
    )
    return (
        step_size,
        projected[:, rank_width : rank_width + states],
        projected[:, rank_width + states :],
    )


def recur(carried, activated, step_size, state_input, state_output, decay_log, skip_gain, accepted):
    decay = -jnp.exp(decay_log)
    accepted_state = carried
    token_outputs = []
    for position in range(activated.shape[1]):
        step_now = step_size[:, position]
        input_now = activated[:, position].astype(jnp.float32)
        carried = (
            jnp.exp(step_now[:, None, :] * decay[None]) * carried
            + (step_now * input_now)[:, None, :] * state_input[:, position, :, None]
        )
        token_outputs.append(
            jnp.einsum("mn,mne->me", state_output[:, position], carried) + skip_gain * input_now
        )
        accepted_state = jnp.where(
            (accepted == position + 1)[:, None, None], carried, accepted_state
        )
    return (
        jnp.stack(token_outputs, axis=1).astype(jnp.bfloat16),
        accepted_state.astype(jnp.bfloat16),
    )


def roll_window(window, accepted, kept_taps):
    selected = window[:, 0:kept_taps]
    for position in range(1, window.shape[1] - kept_taps + 1):
        selected = jnp.where(
            (accepted == position)[:, None, None],
            window[:, position : position + kept_taps],
            selected,
        )
    return selected


def advance(
    start_state,
    earlier_inputs,
    inputs,
    accepted_rows,
    kernel_weight,
    kernel_bias,
    select_weight,
    step_gain,
    step_weight,
    step_bias,
    decay_log,
    skip_gain,
):
    row_count, draft_steps, channels = inputs.shape
    states = decay_log.shape[0]
    activated, window = convolve(inputs, earlier_inputs, kernel_weight, kernel_bias)
    step_size, state_input, state_output = gates(
        activated.reshape(row_count * draft_steps, channels),
        select_weight,
        step_gain,
        step_weight,
        step_bias,
        states,
    )
    outputs, accepted_state = recur(
        start_state.astype(jnp.float32),
        activated,
        step_size.reshape(row_count, draft_steps, channels),
        state_input.reshape(row_count, draft_steps, states),
        state_output.reshape(row_count, draft_steps, states),
        decay_log,
        skip_gain,
        accepted_rows,
    )
    rolled = roll_window(window, accepted_rows, earlier_inputs.shape[1])
    return (outputs, accepted_state, rolled)


def on_device(
    hidden_input,
    input_weight,
    kernel_weight,
    kernel_bias,
    select_weight,
    step_gain,
    step_weight,
    step_bias,
    decay_log,
    skip_gain,
    state_cache,
    window_cache,
    cache_owner,
    cache_slot,
    accepted,
):
    owner_count = lax.axis_size("dp")
    request_count = cache_owner.shape[0]
    capacity = 2 * request_count // owner_count
    slots_here = state_cache.shape[0]
    states = state_cache.shape[1]
    kept_taps = window_cache.shape[1]
    channels = state_cache.shape[2]
    draft_steps = hidden_input.shape[0] // request_count
    matches = (cache_owner[:, None] == jnp.arange(owner_count)[None, :]).astype(jnp.int32)
    within = jnp.sum((jnp.cumsum(matches, axis=0) - matches) * matches, axis=1)
    buffer_row = cache_owner * capacity + within
    inputs = project_input(hidden_input, input_weight).reshape(request_count, draft_steps, channels)
    wanted = (
        jnp.full((owner_count * capacity,), slots_here, jnp.int32)
        .at[buffer_row]
        .set(cache_slot)
        .reshape(owner_count, capacity)
    )
    wanted_slots = lax.all_to_all(wanted, "dp", split_axis=0, concat_axis=0, tiled=True)
    item_count = wanted_slots.shape[1]
    clamped = jnp.minimum(wanted_slots.reshape(-1), slots_here - 1)
    found_states = state_cache[clamped].reshape(owner_count, item_count, states, channels)
    found_windows = window_cache[clamped].reshape(owner_count, item_count, kept_taps, channels)
    found_states, found_windows = (
        lax.all_to_all(found_states, "dp", split_axis=0, concat_axis=0, tiled=True),
        lax.all_to_all(found_windows, "dp", split_axis=0, concat_axis=0, tiled=True),
    )
    start_state = found_states.reshape(owner_count * capacity, states, channels)[buffer_row]
    earlier_inputs = found_windows.reshape(owner_count * capacity, kept_taps, channels)[buffer_row]
    outputs, accepted_state, rolled = advance(
        start_state,
        earlier_inputs,
        inputs,
        accepted,
        kernel_weight,
        kernel_bias,
        select_weight,
        step_gain,
        step_weight,
        step_bias,
        decay_log,
        skip_gain,
    )
    outgoing_states = (
        jnp.zeros((owner_count * capacity, states, channels), jnp.bfloat16)
        .at[buffer_row]
        .set(accepted_state)
        .reshape(owner_count, capacity, states, channels)
    )
    outgoing_windows = (
        jnp.zeros((owner_count * capacity, kept_taps, channels), jnp.bfloat16)
        .at[buffer_row]
        .set(rolled)
        .reshape(owner_count, capacity, kept_taps, channels)
    )
    stored_states, stored_windows = (
        lax.all_to_all(outgoing_states, "dp", split_axis=0, concat_axis=0, tiled=True),
        lax.all_to_all(outgoing_windows, "dp", split_axis=0, concat_axis=0, tiled=True),
    )
    targets = wanted_slots.reshape(-1)
    new_state_cache = state_cache.at[targets].set(
        stored_states.reshape(-1, states, channels), mode="drop"
    )
    new_window_cache = window_cache.at[targets].set(
        stored_windows.reshape(-1, kept_taps, channels), mode="drop"
    )
    return (
        outputs.reshape(request_count * draft_steps, channels),
        new_state_cache,
        new_window_cache,
    )


def solution(mesh):
    in_specs = (
        P(("groups", "dp"), "tensor"),
        P(None, "tensor"),
        P(None, "tensor"),
        P("tensor"),
        P("tensor", None),
        P(),
        P(None, "tensor"),
        P("tensor"),
        P(None, "tensor"),
        P("tensor"),
        P(("groups", "dp"), None, "tensor"),
        P(("groups", "dp"), None, "tensor"),
        P(("groups", "dp")),
        P(("groups", "dp")),
        P(("groups", "dp")),
    )
    out_specs = (
        P(("groups", "dp"), "tensor"),
        P(("groups", "dp"), None, "tensor"),
        P(("groups", "dp"), None, "tensor"),
    )
    return jax.shard_map(
        on_device, mesh=mesh, in_specs=in_specs, out_specs=out_specs, check_vma=False
    )
```

profile of v0, /device:TPU:0, one launch (start us, length us, event | category | flops | bytes accessed | tf_op | source)
XLA Modules:
  0.0 529.0 jit_solution(17720255961756886406)
XLA Ops:
  7.2 1.4 copy.230
  8.6 5.7 %copy.229 = bf16[80,16,2048]{2,1,0:T(8,128)(2,1)} copy(bf16[80,16,2048]{2,1,0:T(8,128)(2,1)} %param.25) | data formatting | bytes 10485760
  14.4 0.2 select_reduce_fusion
  14.6 0.9 scatter_custom_fusion
  15.6 11.7 %all_to_all.29 = s32[4,1,32]{2,1,0:T(1,128)S(1)} all-to-all(s32[4,1,32]{2,1,0:T(1,128)S(1)} %bitcast.155), channel_id=1, replica_groups=mesh['groups'=2,'tensor'=4,'dp'=4] {'dp'}, dimensions={0} | all-to-all | bytes 1024 | tf_op jit(solution)/shard_map/all_to_all | solution.py:154
  27.3 0.5 broadcast.125
  27.8 0.7 reduce.3
  28.5 6.4 %gather_fusion = bf16[128,3,2048]{2,0,1:T(8,128)(2,1)} fusion(bf16[80,3,2048]{2,0,1:T(8,128)(2,1)S(1)} %copy.230, s32[1024]{0:T(1024)S(1)} %pad_clamp_fusion.1), kind=kCustom, calls=%fused_computation | custom fusion | bytes 3146240 | tf_op jit(solution)/shard_map/gather | solution.py:158
  34.9 2.8 copy.149
  37.7 4.4 all-to-all-start.1
  42.1 9.0 %gather_fusion.2 = bf16[128,16,2048]{2,1,0:T(8,128)(2,1)} fusion(bf16[80,16,2048]{2,1,0:T(8,128)(2,1)} %copy.229, s32[1024]{0:T(1024)S(1)} %pad_clamp_fusion.1), kind=kCustom, calls=%fused_computation.2 | custom fusion | bytes 16777728 | tf_op jit(solution)/shard_map/gather | solution.py:157
  51.0 26.9 %all-to-all-done.1 = bf16[4,32,3,2048]{3,1,2,0:T(8,128)(2,1)} async-done(((bf16[4,32,3,2048]{3,1,2,0:T(8,128)(2,1)}), bf16[4,32,3,2048]{3,1,2,0:T(8,128)(2,1)}, u32[]{:S(2)}, u32[]{:S(2)}) %all-to-all-start.1) | async-done | bytes 1572896 | tf_op jit(solution)/shard_map/all_to_all | solution.py:161
  77.9 5.8 %all-to-all-start.2 = ((bf16[4,32,16,2048]{3,2,1,0:T(8,128)(2,1)}), bf16[4,32,16,2048]{3,2,1,0:T(8,128)(2,1)}, u32[]{:S(2)}, u32[]{:S(2)}) async-start(bf16[4,32,16,2048]{3,2,1,0:T(8,128)(2,1)} %bitcast.126), calls=%async_computation.2 | async-start | bytes 16777216 | tf_op jit(solution)/shard_map/all_to_all | solution.py:160
  83.7 0.7 all-gather.2.cloned.1.call-update
  84.6 4.1 copy.150
  88.8 3.9 gather_fusion.1
  92.7 2.8 copy_dynamic-update-slice_fusion
  95.5 26.5 %all-gather.2.cloned.1.call-done = bf16[256,8192]{1,0:T(8,128)(2,1)} async-done(((bf16[256,2048]{1,0:T(8,128)(2,1)}), bf16[256,8192]{1,0:T(8,128)(2,1)}) %all-gather.2.cloned.1.call-update) | async-done | bytes 4194320 | tf_op jit(solution)/shard_map/all_gather | solution.py:11
  122.0 17.2 %convolution_convert_fusion = bf16[256,2048]{1,0:T(8,128)(2,1)} fusion(bf16[256,8192]{1,0:T(8,128)(2,1)} %all-gather.2.cloned.1.call-done, bf16[8192,2048]{1,0:T(8,128)(2,1)} %param.16), kind=kOutput, calls=%fused_computation.39 | convolution fusion | flops 8590458880 | bytes 38797312 | tf_op jit(solution)/shard_map/dot_general | solution.py:10
  139.2 2.2 reshape.142
  141.5 3.2 fusion.56
  144.6 3.6 multiply_convert_fusion
  148.3 1.1 copy-done.3
  149.3 1.8 copy.154
  151.2 2.1 reshape.143
  153.3 2.8 fusion.60
  156.2 3.2 fusion.26
  159.4 1.6 copy.177
  161.1 1.0 broadcast_in_dim.95
  162.1 6.4 %scatter_fusion.2 = bf16[128,3,2048]{2,1,0:T(4,128)(2,1)S(1)} fusion(bf16[128,3,2048]{2,1,0:T(4,128)(2,1)S(1)} %broadcast_in_dim.95, s32[64]{0:T(128)S(1)} %compare_select_fusion.3, bf16[64,3,2048]{2,1,0:T(4,128)(2,1)} %copy.177), kind=kCustom, calls=%fused_computation.7 | custom fusion | bytes 2359552 | tf_op jit(solution)/shard_map/scatter | solution.py:188
  168.5 2.3 copy.178
  170.9 18.8 %all-reduce.2.cloned.1.call-done = f32[256,544]{0,1:T(8,128)} async-done(((f32[256,544]{0,1:T(8,128)}), f32[256,544]{0,1:T(8,128)}) %all-reduce.2.cloned.1.call-update) | async-done | bytes 557072 | tf_op jit(solution)/shard_map/psum | solution.py:31
  189.7 0.7 slice.136
  190.4 0.1 copy.158
  190.5 1.1 multiply_reduce_fusion
  191.7 4.9 compare_select_fusion
  196.6 2.8 reshape.145
  199.5 6.9 %fusion.55 = (f32[64,1,2048]{2,1,0:T(1,128)S(1)}, f32[64,1,2048]{2,1,0:T(1,128)S(1)}, f32[64,1,2048]{2,1,0:T(1,128)}, f32[64,1,2048]{2,1,0:T(1,128)}) fusion(f32[64,4,2048]{2,1,0:T(4,128)} %reshape.145), kind=kLoop, calls=%fused_computation.103 | loop fusion | bytes 4194304 | tf_op jit(solution)/shard_map/slice | solution.py:51
  206.4 59.9 %all-to-all-done.2 = bf16[4,32,16,2048]{3,2,1,0:T(8,128)(2,1)} async-done(((bf16[4,32,16,2048]{3,2,1,0:T(8,128)(2,1)}), bf16[4,32,16,2048]{3,2,1,0:T(8,128)(2,1)}, u32[]{:S(2)}, u32[]{:S(2)}) %all-to-all-start.2) | async-done | bytes 8388640 | tf_op jit(solution)/shard_map/all_to_all | solution.py:160
  266.3 4.4 all-to-all-start.4
  270.8 3.5 fusion.27
  274.3 6.2 %gather_fusion.3 = bf16[64,16,2048]{2,1,0:T(8,128)(2,1)} fusion(bf16[128,16,2048]{2,1,0:T(8,128)(2,1)} %bitcast.13, s32[1024]{0:T(1024)S(1)} %pad_clamp_fusion), kind=kCustom, calls=%fused_computation.3 | custom fusion | bytes 8388864 | tf_op jit(solution)/shard_map/gather | solution.py:163
  280.6 14.5 %fusion.4 = bf16[64,16,2048]{2,1,0:T(8,128)(2,1)} fusion(bf16[64,16,2048]{2,1,0:T(8,128)(2,1)} %gather_fusion.3, f32[64,16]{1,0:T(8,128)S(1)} %bitcast.142, f32[64,2048]{1,0:T(8,128)S(1)} %copy-done.7, f32[64,2048]{1,0:T(8,128)} %get-tuple-element.19, f32[64,16]{1,0:T(8,128)S(1)} %bitcast.144, f32[64,2048]{1,0:T(8,128)} %get-tuple-element.15, ...), kind=kLoop, calls=%fused_computation.15 | loop fusion | flops 46137344 | bytes 12730624 | tf_op jit(solution)/shard_map/convert_element_type | solution.py:65
  295.1 4.3 broadcast_in_dim.90
  299.3 12.0 %scatter_fusion = bf16[128,16,2048]{2,1,0:T(8,128)(2,1)} fusion(bf16[128,16,2048]{2,1,0:T(8,128)(2,1)} %broadcast_in_dim.90, s32[64]{0:T(128)S(1)} %compare_select_fusion.3, bf16[64,16,2048]{2,1,0:T(8,128)(2,1)} %fusion.4), kind=kCustom, calls=%fused_computation.5 | custom fusion | bytes 12583168 | tf_op jit(solution)/shard_map/scatter | solution.py:182
  311.4 5.9 %all-to-all-start.3 = ((bf16[4,32,16,2048]{3,2,1,0:T(8,128)(2,1)}), bf16[4,32,16,2048]{3,2,1,0:T(8,128)(2,1)}, u32[]{:S(2)}, u32[]{:S(2)}) async-start(bf16[4,32,16,2048]{3,2,1,0:T(8,128)(2,1)} %bitcast.125), calls=%async_computation.3 | async-start | bytes 16777216 | tf_op jit(solution)/shard_map/all_to_all | solution.py:192
  317.2 0.7 slice.131
  318.0 0.1 copy.155
  318.5 0.1 copy.182
  318.6 0.1 copy.184
  318.8 0.1 copy.186
  318.9 0.1 copy.180
  319.0 2.8 copy.179
  321.7 33.9 %scatter_fusion.3 = bf16[80,3,2048]{2,0,1:T(8,128)(2,1)S(1)} fusion(bf16[80,3,2048]{2,0,1:T(8,128)(2,1)S(1)} %copy.230, s32[128]{0:T(128)S(1)} %get-tuple-element.37, bf16[128,3,2048]{2,0,1:T(8,128)(2,1)} %bitcast.128), kind=kCustom, calls=%fused_computation.8 | custom fusion | bytes 4719104 | tf_op jit(solution)/shard_map/scatter | solution.py:199
  355.7 4.9 fusion.6
  360.6 4.3 fusion.54
  364.9 5.9 %fusion.8 = f32[64,1,2048]{2,1,0:T(1,128)S(1)} fusion(bf16[64,16,1]{1,2,0:T(2,128)(2,1)S(1)} %copy.184, f32[64,16]{1,0:T(8,128)S(1)} %bitcast.145, f32[64,2048]{1,0:T(8,128)S(1)} %copy-done.8, f32[64,2048]{1,0:T(8,128)S(1)} %copy-done.11, f32[16,2048]{1,0:T(8,128)S(1)} %exponential_negate_fusion, bf16[64,16,2048]{2,1,0:T(8,128)(2,1)S(1)} %copy-done.5, ...), kind=kOutput, calls=%fused_computation.21 | convolution fusion | flops 31457280 | bytes 8009728 | tf_op jit(solution)/shard_map/mn,mne->me/dot_general | solution.py:58
  370.8 8.1 %fusion.5 = f32[64,1,2048]{2,1,0:T(1,128)S(1)} fusion(bf16[64,16,1]{1,2,0:T(2,128)(2,1)S(1)} %copy.186, f32[64,16]{1,0:T(8,128)S(1)} %bitcast.143, f32[64,2048]{1,0:T(8,128)S(1)} %copy-done.7, f32[64,2048]{1,0:T(8,128)S(1)} %copy-done.12, f32[64,16]{1,0:T(8,128)S(1)} %bitcast.146, f32[64,2048]{1,0:T(8,128)S(1)} %copy-done.8, f32[64,2048]{1,0:T(8,128)S(1)} %copy-done.11, ...), kind=kOutput, calls=%fused_computation.17 | convolution fusion | flops 39845888 | bytes 9062400 | tf_op jit(solution)/shard_map/mn,mne->me/dot_general | solution.py:58
  379.0 1.1 fusion.46
  380.1 0.1 pad_maximum_fusion
  380.2 0.8 copy.173
  381.0 1.1 convert_element_type.92
  382.1 117.7 %all-to-all-done.3 = bf16[4,32,16,2048]{3,2,1,0:T(8,128)(2,1)} async-done(((bf16[4,32,16,2048]{3,2,1,0:T(8,128)(2,1)}), bf16[4,32,16,2048]{3,2,1,0:T(8,128)(2,1)}, u32[]{:S(2)}, u32[]{:S(2)}) %all-to-all-start.3) | async-done | bytes 8388640 | tf_op jit(solution)/shard_map/all_to_all | solution.py:192
  499.9 21.9 %scatter_fusion.1 = bf16[80,16,2048]{2,1,0:T(8,128)(2,1)} fusion(bf16[80,16,2048]{2,1,0:T(8,128)(2,1)} %copy.229, s32[128]{0:T(128)S(1)} %get-tuple-element.37, bf16[128,16,2048]{2,1,0:T(8,128)(2,1)} %bitcast.46), kind=kCustom, calls=%fused_computation.6 | custom fusion | bytes 25166336 | tf_op jit(solution)/shard_map/scatter | solution.py:196
  (77 shorter events, 1.2 us)
Async XLA Ops:
  7.2 146.1 %copy-start = (bf16[2048,544]{0,1:T(8,128)(2,1)S(1)}, bf16[2048,544]{0,1:T(8,128)(2,1)}, u32[]{:S(2)}) copy-start(bf16[2048,544]{0,1:T(8,128)(2,1)} %param.19) | copy-start | bytes 6684676
  7.2 7.1 %copy-start.18 = (s32[64]{0:T(128)S(1)}, s32[64]{0:T(128)}, u32[]{:S(2)}) copy-start(s32[64]{0:T(128)} %param.27) | copy-start | bytes 772
  37.7 40.2 %all-to-all-start.1 = ((bf16[4,32,3,2048]{3,1,2,0:T(8,128)(2,1)}), bf16[4,32,3,2048]{3,1,2,0:T(8,128)(2,1)}, u32[]{:S(2)}, u32[]{:S(2)}) async-start(bf16[4,32,3,2048]{3,1,2,0:T(8,128)(2,1)} %copy.149), calls=%async_computation.1 | async-start | bytes 3145728 | tf_op jit(solution)/shard_map/all_to_all | solution.py:161
  77.9 6.6 %copy-start.25 = (s32[64]{0:T(128)S(1)}, s32[64]{0:T(128)}, u32[]{:S(2)}) copy-start(s32[64]{0:T(128)} %param.29) | copy-start | bytes 772
  77.9 6.6 %copy-start.15 = (f32[4,2048]{1,0:T(4,128)S(1)}, f32[4,2048]{1,0:T(4,128)}, u32[]{:S(2)}) copy-start(f32[4,2048]{1,0:T(4,128)} %param.17) | copy-start | bytes 98308
  77.9 6.7 %copy-start.14 = (f32[16,2048]{1,0:T(8,128)S(1)}, f32[16,2048]{1,0:T(8,128)}, u32[]{:S(2)}) copy-start(f32[16,2048]{1,0:T(8,128)} %param.23) | copy-start | bytes 393220
  77.9 188.3 %all-to-all-start.2 = ((bf16[4,32,16,2048]{3,2,1,0:T(8,128)(2,1)}), bf16[4,32,16,2048]{3,2,1,0:T(8,128)(2,1)}, u32[]{:S(2)}, u32[]{:S(2)}) async-start(bf16[4,32,16,2048]{3,2,1,0:T(8,128)(2,1)} %bitcast.126), calls=%async_computation.2 | async-start | bytes 16777216 | tf_op jit(solution)/shard_map/all_to_all | solution.py:160
  83.7 38.3 %all-gather.2.cloned.1.call-start = ((), (), s32[]{:S(2)}) async-start(), calls=%async_computation.5 | async-start | bytes 5242880 | tf_op jit(solution)/shard_map/all_gather | solution.py:11
  84.4 105.3 %all-reduce.2.cloned.1.call-start = ((), (), s32[]{:S(2)}) async-start(), calls=%async_computation.6 | async-start | bytes 1114112 | tf_op jit(solution)/shard_map/psum | solution.py:31
  84.5 71.6 %copy-start.19 = (pred[64]{0:T(512)(128)(4,1)}, pred[64]{0:T(512)(128)(4,1)S(1)}, u32[]{:S(2)}) copy-start(pred[64]{0:T(512)(128)(4,1)S(1)} %get-tuple-element.34) | copy-start | bytes 196
  84.5 71.6 %copy-start.21 = (pred[64]{0:T(512)(128)(4,1)}, pred[64]{0:T(512)(128)(4,1)S(1)}, u32[]{:S(2)}) copy-start(pred[64]{0:T(512)(128)(4,1)S(1)} %get-tuple-element.35) | copy-start | bytes 196
  84.6 71.6 %copy-start.23 = (pred[64]{0:T(512)(128)(4,1)}, pred[64]{0:T(512)(128)(4,1)S(1)}, u32[]{:S(2)}) copy-start(pred[64]{0:T(512)(128)(4,1)S(1)} %get-tuple-element.36) | copy-start | bytes 196
  95.5 49.2 %copy-start.16 = (f32[2048]{0:T(1024)S(1)}, f32[2048]{0:T(1024)}, u32[]{:S(2)}) copy-start(f32[2048]{0:T(1024)} %param.18) | copy-start | bytes 24580
  148.3 1.1 copy-start.3
  156.1 35.5 %copy-start.26 = (f32[2048]{0:T(1024)S(1)}, f32[2048]{0:T(1024)}, u32[]{:S(2)}) copy-start(f32[2048]{0:T(1024)} %param.22) | copy-start | bytes 24580
  156.1 35.5 %copy-start.27 = (f32[512]{0:T(512)S(1)}, f32[512]{0:T(512)}, u32[]{:S(2)}) copy-start(f32[512]{0:T(512)} %param.20) | copy-start | bytes 6148
  191.7 79.1 %copy-start.4 = (bf16[64,4,2048]{2,0,1:T(8,128)(2,1)S(1)}, bf16[64,4,2048]{2,0,1:T(8,128)(2,1)}, u32[]{:S(2)}) copy-start(bf16[64,4,2048]{2,0,1:T(8,128)(2,1)} %copy-done.3) | copy-start | bytes 3145732
  266.3 45.1 %all-to-all-start.4 = ((bf16[4,32,3,2048]{3,1,2,0:T(8,128)(2,1)}), bf16[4,32,3,2048]{3,1,2,0:T(8,128)(2,1)}, u32[]{:S(2)}, u32[]{:S(2)}) async-start(bf16[4,32,3,2048]{3,1,2,0:T(8,128)(2,1)} %copy.178), calls=%async_computation.4 | async-start | bytes 3145728 | tf_op jit(solution)/shard_map/all_to_all | solution.py:193
  270.6 9.9 %copy-start.20 = (pred[64]{0:T(512)(128)(4,1)S(1)}, pred[64]{0:T(512)(128)(4,1)}, u32[]{:S(2)}) copy-start(pred[64]{0:T(512)(128)(4,1)} %copy-done.19) | copy-start | bytes 196
  270.7 9.9 %copy-start.22 = (pred[64]{0:T(512)(128)(4,1)S(1)}, pred[64]{0:T(512)(128)(4,1)}, u32[]{:S(2)}) copy-start(pred[64]{0:T(512)(128)(4,1)} %copy-done.21) | copy-start | bytes 196
  270.7 9.9 %copy-start.24 = (pred[64]{0:T(512)(128)(4,1)S(1)}, pred[64]{0:T(512)(128)(4,1)}, u32[]{:S(2)}) copy-start(pred[64]{0:T(512)(128)(4,1)} %copy-done.23) | copy-start | bytes 196
  274.3 6.2 %copy-start.6 = (f32[64,2048]{1,0:T(8,128)S(1)}, f32[64,2048]{1,0:T(8,128)}, u32[]{:S(2)}) copy-start(f32[64,2048]{1,0:T(8,128)} %get-tuple-element.13) | copy-start | bytes 1572868
  274.3 6.3 %copy-start.7 = (f32[64,2048]{1,0:T(8,128)S(1)}, f32[64,2048]{1,0:T(8,128)}, u32[]{:S(2)}) copy-start(f32[64,2048]{1,0:T(8,128)} %get-tuple-element.14) | copy-start | bytes 1572868
  311.4 188.5 %all-to-all-start.3 = ((bf16[4,32,16,2048]{3,2,1,0:T(8,128)(2,1)}), bf16[4,32,16,2048]{3,2,1,0:T(8,128)(2,1)}, u32[]{:S(2)}, u32[]{:S(2)}) async-start(bf16[4,32,16,2048]{3,2,1,0:T(8,128)(2,1)} %bitcast.125), calls=%async_computation.3 | async-start | bytes 16777216 | tf_op jit(solution)/shard_map/all_to_all | solution.py:192
  355.6 9.2 %copy-start.2 = (bf16[80,3,2048]{2,0,1:T(8,128)(2,1)}, bf16[80,3,2048]{2,0,1:T(8,128)(2,1)S(1)}, u32[]{:S(2)}) copy-start(bf16[80,3,2048]{2,0,1:T(8,128)(2,1)S(1)} %scatter_fusion.3) | copy-start | bytes 2949124
  355.6 4.9 copy-start.5
  355.7 4.9 copy-start.9
  355.7 4.9 copy-start.10
  355.7 4.9 copy-start.13
  360.6 4.3 copy-start.8
  360.6 4.3 copy-start.11
  364.9 5.9 %copy-start.12 = (f32[64,2048]{1,0:T(8,128)S(1)}, f32[64,2048]{1,0:T(8,128)}, u32[]{:S(2)}) copy-start(f32[64,2048]{1,0:T(8,128)} %get-tuple-element.19) | copy-start | bytes 1572868
  370.8 8.1 %copy-start.17 = (f32[2048]{0:T(1024)S(1)}, f32[2048]{0:T(1024)}, u32[]{:S(2)}) copy-start(f32[2048]{0:T(1024)} %param.24) | copy-start | bytes 24580
  499.9 21.9 %copy-start.1 = (bf16[2048,544]{0,1:T(8,128)(2,1)S(1)}, bf16[2048,544]{0,1:T(8,128)(2,1)}, u32[]{:S(2)}) copy-start(bf16[2048,544]{0,1:T(8,128)(2,1)} %param.19) | copy-start | bytes 6684676
Sparse Core Ops, SparseCore 0:
  86.1 35.8 all-gather.1
  156.3 33.3 all-reduce.1
where the time goes:
time: 539 us; the launch traced here: 529 us
  waiting for transfers between devices  251 us (47%)
  local copies, waits for them, and re-layouts  155 us (29%)
  matrix products  48.1 us (9%)
  other arithmetic  28.3 us (5%)
  starting transfers between devices  20.4 us (4%)
  between operations  15 us (3%)
  blocking collectives  11.7 us (2%)
    all_to_all x1, waiting for transfers between devices, on_device(): lax.all_to_all(outgoing_states, 'dp', split_axis=0, concat_axis=0, tiled=...  118 us
    all_to_all x1, waiting for transfers between devices, on_device(): lax.all_to_all(found_states, 'dp', split_axis=0, concat_axis=0, tiled=True)  59.9 us
    scatter x1, local copies, waits for them, and re-layouts, on_device(): window_cache.at[targets]  33.9 us
    all_to_all x1, waiting for transfers between devices, on_device(): lax.all_to_all(found_windows, 'dp', split_axis=0, concat_axis=0, tiled=True)  26.9 us
    all_gather x1, waiting for transfers between devices, project_input(): lax.all_gather(hidden_input, 'tensor', axis=1, tiled=True)  26.5 us
    dot_general x4, matrix products, recur(): jnp.einsum('mn,mne->me', state_output[:, position], carried)  23.2 us
    scatter x1, local copies, waits for them, and re-layouts, on_device(): state_cache.at[targets]  21.9 us
    psum x1, waiting for transfers between devices, gates(): projected = lax.psum(partial_value, 'tensor')  18.8 us
  transfers between devices with their start and end apart: 6, of which 5 were waited for; matrix products, arithmetic and copies ran while one was open for 36% of the time, Pallas kernels for 0%

commit v1 on v0

v1 whole, which is shorter than its diff:
```python
import jax
import jax.numpy as jnp
from jax import lax
from jax.sharding import PartitionSpec as P

epsilon = 1e-06


def one_hot_rows(row_code, column_code):
    return (row_code[:, None] == column_code[None, :]).astype(jnp.bfloat16)


def move_rows(selector, rows):
    return jnp.dot(selector, rows, preferred_element_type=jnp.float32).astype(jnp.bfloat16)


def routing(cache_owner, cache_slot, accepted, slots_here):
    owner_count = lax.axis_size("dp")
    here = lax.axis_index("dp")
    request_count = cache_owner.shape[0]
    capacity = 2 * request_count // owner_count
    place = cache_owner * slots_here + cache_slot
    everyone = lax.all_gather(place * 8 + accepted, "dp", axis=0, tiled=False)
    earlier = jnp.tril(jnp.ones((request_count, request_count), jnp.int32), -1)
    place_all = everyone // 8
    owner_all = place_all // slots_here
    same = (owner_all[:, :, None] == owner_all[:, None, :]).astype(jnp.int32)
    within_all = jnp.sum(same * earlier[None], axis=2)
    mine = (owner_all == here).reshape(-1)
    slot_all = jnp.where(mine, (place_all - here * slots_here).reshape(-1), -1)
    packed_all = (jnp.arange(owner_count)[:, None] * capacity + within_all).reshape(-1)
    match = slot_all[None, :] == jnp.arange(slots_here)[:, None]
    slot_source = jnp.max(jnp.where(match, packed_all[None, :], -1), axis=1)
    slot_accepted = jnp.max(jnp.where(match, (everyone % 8).reshape(-1)[None, :], 0), axis=1)
    own_same = (cache_owner[:, None] == cache_owner[None, :]).astype(jnp.int32)
    send_row = cache_owner * capacity + jnp.sum(own_same * earlier, axis=1)
    return send_row, slot_source, slot_accepted, capacity


def on_device(
    hidden_input,
    input_weight,
    kernel_weight,
    kernel_bias,
    select_weight,
    step_gain,
    step_weight,
    step_bias,
    decay_log,
    skip_gain,
    state_cache,
    window_cache,
    cache_owner,
    cache_slot,
    accepted,
):
    owner_count = lax.axis_size("dp")
    slots, states, channels = state_cache.shape
    kept = window_cache.shape[1]
    request_count = cache_owner.shape[0]
    tokens = hidden_input.shape[0] // request_count
    send_row, slot_source, slot_accepted, capacity = routing(
        cache_owner, cache_slot, accepted, slots
    )
    packed = owner_count * capacity
    token_axis = jnp.arange(tokens, dtype=jnp.int32)
    request_code = (send_row[:, None] * tokens + token_axis[None, :]).reshape(-1)
    packed_index = jnp.arange(packed, dtype=jnp.int32).reshape(owner_count, 1, capacity)
    packed_code = (packed_index * tokens + token_axis[None, :, None]).reshape(-1)
    slot_code = jnp.where(
        slot_source[None, :] >= 0, slot_source[None, :] * tokens + token_axis[:, None], -1
    ).reshape(-1)

    outgoing = move_rows(one_hot_rows(packed_code, request_code), hidden_input)
    outgoing = outgoing.reshape(owner_count, tokens * capacity, -1)
    arrived = lax.all_to_all(outgoing, "dp", split_axis=0, concat_axis=0, tiled=True)
    placed = move_rows(
        one_hot_rows(slot_code, packed_code), arrived.reshape(packed * tokens, -1)
    )
    gathered = lax.all_gather(placed, "tensor", axis=1, tiled=True)
    inputs = jnp.dot(gathered, input_weight, preferred_element_type=jnp.float32).astype(
        jnp.bfloat16
    ).reshape(tokens, slots, channels)
    old_window = jnp.transpose(window_cache, (1, 0, 2))
    window = jnp.concatenate([old_window, inputs], axis=0)
    mixed = kernel_bias + kernel_weight[0] * window[0:tokens].astype(jnp.float32)
    for tap in range(1, kernel_weight.shape[0]):
        mixed = mixed + kernel_weight[tap] * window[tap : tap + tokens].astype(jnp.float32)
    activated = jax.nn.silu(mixed).astype(jnp.bfloat16)
    rolled = window[0:kept]
    for position in range(1, tokens + 1):
        rolled = jnp.where(
            (slot_accepted == position)[None, :, None], window[position : position + kept], rolled
        )
    new_window_cache = jnp.transpose(rolled, (1, 0, 2))

    partial_value = jnp.dot(
        activated.reshape(tokens * slots, channels),
        select_weight,
        preferred_element_type=jnp.float32,
    )
    projected = lax.psum(partial_value, "tensor")
    rank = step_gain.shape[0]
    rank_part = projected[:, :rank]
    norm_scale = lax.rsqrt(jnp.mean(rank_part * rank_part, axis=1, keepdims=True) + epsilon)
    rank_normed = (rank_part * norm_scale * step_gain).astype(jnp.bfloat16)
    step_size = jax.nn.softplus(
        jnp.dot(rank_normed, step_weight, preferred_element_type=jnp.float32) + step_bias
    ).reshape(tokens, slots, channels)
    state_input = projected[:, rank : rank + states].reshape(tokens, slots, states)
    state_output = projected[:, rank + states :].reshape(tokens, slots, states)

    decay = -jnp.exp(decay_log)
    carried = state_cache.astype(jnp.float32)
    kept_state = carried
    outputs = []
    for t in range(tokens):
        step_now = step_size[t]
        input_now = activated[t].astype(jnp.float32)
        carried = (
            jnp.exp(step_now[:, None, :] * decay[None]) * carried
            + (step_now * input_now)[:, None, :] * state_input[t][:, :, None]
        )
        outputs.append(
            jnp.sum(state_output[t][:, :, None] * carried, axis=1) + skip_gain * input_now
        )
        kept_state = jnp.where((slot_accepted == t + 1)[:, None, None], carried, kept_state)
    new_state_cache = kept_state.astype(jnp.bfloat16)
    outputs = jnp.stack(outputs, axis=0).astype(jnp.bfloat16).reshape(tokens * slots, channels)

    returning = move_rows(one_hot_rows(packed_code, slot_code), outputs)
    returning = returning.reshape(owner_count, tokens * capacity, channels)
    returned = lax.all_to_all(returning, "dp", split_axis=0, concat_axis=0, tiled=True)
    mamba_output = move_rows(
        one_hot_rows(request_code, packed_code), returned.reshape(packed * tokens, channels)
    )
    return mamba_output, new_state_cache, new_window_cache


def solution(mesh):
    in_specs = (
        P(("groups", "dp"), "tensor"),
        P(None, "tensor"),
        P(None, "tensor"),
        P("tensor"),
        P("tensor", None),
        P(),
        P(None, "tensor"),
        P("tensor"),
        P(None, "tensor"),
        P("tensor"),
        P(("groups", "dp"), None, "tensor"),
        P(("groups", "dp"), None, "tensor"),
        P(("groups", "dp")),
        P(("groups", "dp")),
        P(("groups", "dp")),
    )
    out_specs = (
        P(("groups", "dp"), "tensor"),
        P(("groups", "dp"), None, "tensor"),
        P(("groups", "dp"), None, "tensor"),
    )
    return jax.shard_map(
        on_device, mesh=mesh, in_specs=in_specs, out_specs=out_specs, check_vma=False
    )
```

time: 539 us -> 271 us (0.50); the launches traced: 529 us -> 270 us
  waiting for transfers between devices: 251 us -> 98.1 us
  local copies, waits for them, and re-layouts: 155 us -> 8.27 us
  blocking collectives: 11.7 us -> 48.4 us
  other arithmetic: 28.3 us -> 51.1 us
  matrix products: 48.1 us -> 37.3 us
  starting transfers between devices: 20.4 us -> 11.2 us
    all_to_all x4 -> x2, waiting for transfers between devices: 204 us -> 25.8 us  [the longest x1 25.8 us: on_device(): lax.all_to_all(returning, 'dp', split_axis=0, concat_axis=0, tiled=True)]
    scatter x5 -> x0, local copies, waits for them, and re-layouts: 75.1 us -> none  [the longest x1 33.9 us: on_device(): window_cache.at[targets]]
    unnamed x0 -> x1, blocking collectives: none -> 48.4 us
    gather x4 -> x0, local copies, waits for them, and re-layouts: 25.5 us -> none  [the longest x1 8.96 us: on_device(): state_cache[clamped].reshape(owner_count, item_count, states, channels)]
    reduce_sum x2 -> x3, other arithmetic: 1.3 us -> 25.9 us  [the longest x1 24.5 us: on_device(): jnp.sum(state_output[t][:, :, None] * carried, axis=1)]
    reshape x7 -> x0, local copies, waits for them, and re-layouts: 15.6 us -> none  [the longest x2 5.44 us: on_device(): project_input(hidden_input, input_weight)]
    psum x1, waiting for transfers between devices: 18.8 us -> 34 us  [on_device(): projected = lax.psum(partial_value, 'tensor')]
    all_gather x1, waiting for transfers between devices: 26.5 us -> 38.3 us  [on_device(): gathered = lax.all_gather(placed, 'tensor', axis=1, tiled=True)]
  transfers between devices with their start and end apart: 6 -> 4, of which waited for: 5 -> 3; matrix products, arithmetic and copies ran while one was open for 36% -> 8% of each run, Pallas kernels for 0% -> 0%
where the time goes in v1:
time: 271 us; the launch traced here: 270 us
  waiting for transfers between devices  98.1 us (36%)
  other arithmetic  51.1 us (19%)
  blocking collectives  48.4 us (18%)
  matrix products  37.3 us (14%)
  between operations  15.4 us (6%)
  starting transfers between devices  11.2 us (4%)
  local copies, waits for them, and re-layouts  8.27 us (3%)
    unnamed x1, blocking collectives  48.4 us
    all_gather x1, waiting for transfers between devices, on_device(): gathered = lax.all_gather(placed, 'tensor', axis=1, tiled=True)  38.3 us
    psum x1, waiting for transfers between devices, on_device(): projected = lax.psum(partial_value, 'tensor')  34 us
    all_to_all x1, waiting for transfers between devices, on_device(): lax.all_to_all(returning, 'dp', split_axis=0, concat_axis=0, tiled=True)  25.8 us
    reduce_sum x1, other arithmetic, on_device(): jnp.sum(state_output[t][:, :, None] * carried, axis=1)  24.5 us
    dot_general x1, matrix products, on_device(): jnp.dot(gathered, input_weight, preferred_element_type=jnp.float32)  18.5 us
    convert_element_type x1, other arithmetic, on_device(): new_state_cache = kept_state.astype(jnp.bfloat16)  17.4 us
    dot_general x4, matrix products, move_rows(): jnp.dot(selector, rows, preferred_element_type=jnp.float32)  12.8 us
  transfers between devices with their start and end apart: 4, of which 3 were waited for; matrix products, arithmetic and copies ran while one was open for 8% of the time, Pallas kernels for 0%

profile of v1, /device:TPU:0, one launch (start us, length us, event | category | flops | bytes accessed | tf_op | source)
XLA Modules:
  0.0 269.9 jit_solution(13955400920591890154)
XLA Ops:
  7.2 0.0 copy-start
  7.2 1.4 dynamic-slice
  9.3 0.9 fusion.40
  10.2 0.8 add_dynamic-update-slice_fusion
  11.0 0.1 iota_add_fusion
  11.1 0.1 add.226
  11.2 0.1 add.230
  11.3 3.3 %convolution_convert_fusion = bf16[512,2048]{1,0:T(8,128)(2,1)} fusion(bf16[256,2048]{1,0:T(8,128)(2,1)} %param.15, s32[256]{0:T(256)S(1)} %add.226, s32[512]{0:T(512)S(1)} %add.230), kind=kOutput, calls=%fused_computation.19 | convolution fusion | flops 538050560 | bytes 3148800 | tf_op jit(solution)/shard_map/dot_general | solution.py:14
  14.6 6.3 %all-to-all-start = ((bf16[4,128,2048]{2,1,0:T(8,128)(2,1)}), bf16[4,128,2048]{2,1,0:T(8,128)(2,1)}, u32[]{:S(2)}, u32[]{:S(2)}) async-start(bf16[4,128,2048]{2,1,0:T(8,128)(2,1)} %bitcast.53), calls=%async_computation | async-start | bytes 4194304 | tf_op jit(solution)/shard_map/all_to_all | solution.py:76
  20.9 48.4 %all-reduce = s32[256]{0:T(256)S(1)} all-reduce(s32[256]{0:T(256)S(1)} %get-tuple-element.44), channel_id=2, replica_groups=mesh['groups'=2,'tensor'=4,'dp'=4] {'dp'}, use_global_device_ids=true, to_apply=%add | all-reduce | flops 256 | bytes 2048
  69.3 0.1 reshape.373
  69.4 0.1 broadcast_in_dim.133
  69.5 0.1 select_n.92
  69.6 0.2 select_reduce_fusion
  69.8 0.1 broadcast_add_fusion
  69.9 0.1 add.235
  70.0 0.1 select_reduce_fusion.1
  70.2 0.1 select_n.95
  70.2 0.0 all-to-all-done
  70.3 0.0 copy-start.34
  70.3 3.5 %convolution_convert_fusion.2 = bf16[320,2048]{1,0:T(8,128)(2,1)} fusion(bf16[512,2048]{1,0:T(8,128)(2,1)} %bitcast.4, s32[512]{0:T(512)S(1)} %add.230, s32[320]{0:T(512)S(1)} %select_n.95), kind=kOutput, calls=%fused_computation.26 | convolution fusion | flops 671907840 | bytes 3411200 | tf_op jit(solution)/shard_map/dot_general | solution.py:14
  73.8 0.0 all-gather.3.cloned.1.call-update
  73.8 0.2 all-reduce.3.cloned.1.call-start
  74.1 0.6 broadcast_compare_fusion.4
  74.6 0.6 fusion.45
  75.3 38.3 %all-gather.3.cloned.1.call-done = bf16[320,8192]{1,0:T(8,128)(2,1)} async-done(((bf16[320,2048]{1,0:T(8,128)(2,1)}), bf16[320,8192]{1,0:T(8,128)(2,1)}) %all-gather.3.cloned.1.call-update) | async-done | bytes 5242896 | tf_op jit(solution)/shard_map/all_gather | solution.py:80
  113.6 18.5 %convolution_convert_fusion.3 = bf16[320,2048]{1,0:T(8,128)(2,1)S(1)} fusion(bf16[320,8192]{1,0:T(8,128)(2,1)} %all-gather.3.cloned.1.call-done, bf16[8192,2048]{1,0:T(8,128)(2,1)} %param.16), kind=kOutput, calls=%fused_computation.27 | convolution fusion | flops 10738073600 | bytes 40108032 | tf_op jit(solution)/shard_map/dot_general | solution.py:81
  132.1 1.6 multiply_convert_fusion
  133.7 0.0 copy-start.2
  133.7 1.0 copy-done.2
  134.8 2.2 fusion.46
  136.9 0.0 all-reduce.3.cloned.1.call-update
  137.0 0.9 exponential_negate_fusion
  137.9 34.0 %all-reduce.3.cloned.1.call-done = f32[320,544]{1,0:T(8,128)} async-done(((f32[320,544]{1,0:T(8,128)}), f32[320,544]{1,0:T(8,128)}) %all-reduce.3.cloned.1.call-update) | async-done | bytes 696336 | tf_op jit(solution)/shard_map/psum | solution.py:102
  171.9 1.2 multiply_reduce_fusion.4
  173.2 0.0 copy-start.3
  173.2 3.9 %compare_select_fusion = f32[320,2048]{1,0:T(8,128)S(1)} fusion(bf16[512,2048]{1,0:T(8,128)(2,1)} %param.21, f32[2048]{0:T(1024)S(1)} %copy-done.47, f32[320,544]{1,0:T(8,128)} %all-reduce.3.cloned.1.call-done, f32[512]{0:T(512)S(1)} %copy-done.48, f32[320]{0:T(512)S(1)} %add_rsqrt_fusion), kind=kOutput, calls=%fused_computation.14 | convolution fusion | flops 676167680 | bytes 5385472 | tf_op jit(solution)/shard_map/dot_general | solution.py:108
  177.1 0.7 fusion.24
  177.8 0.0 copy-start.6
  177.8 0.0 copy-start.14
  177.9 1.4 fusion.44
  179.4 0.0 copy-start.40
  179.4 24.5 %multiply_reduce_fusion.1 = (f32[80,2048]{1,0:T(8,128)S(1)}, f32[80,2048]{1,0:T(8,128)S(1)}, f32[80,2048]{1,0:T(8,128)S(1)}, f32[80,2048]{1,0:T(8,128)S(1)}) fusion(f32[80,16]{1,0:T(8,128)S(1)} %get-tuple-element.28, f32[80,2048]{1,0:T(8,128)S(1)} %get-tuple-element.12, f32[80,2048]{1,0:T(8,128)S(1)} %get-tuple-element.16, ...), kind=kLoop, calls=%fused_computation.9 | loop fusion | flops 64880640 | bytes 13279232 | tf_op jit(solution)/shard_map/reduce_sum | solution.py:125
  204.0 0.4 fusion.17
  204.5 0.2 pad_maximum_fusion
  204.7 0.5 copy-done.36
  205.1 0.0 copy-done.46
  205.1 2.6 convolution_convert_fusion.1
  207.8 4.7 %all-to-all-start.1 = ((bf16[4,128,2048]{2,1,0:T(8,128)(2,1)}), bf16[4,128,2048]{2,1,0:T(8,128)(2,1)}, u32[]{:S(2)}, u32[]{:S(2)}) async-start(bf16[4,128,2048]{2,1,0:T(8,128)(2,1)} %bitcast.19), calls=%async_computation.1 | async-start | bytes 4194304 | tf_op jit(solution)/shard_map/all_to_all | solution.py:133
  212.5 0.0 copy-start.5
  212.6 0.2 fusion.43
  212.8 0.9 copy-done.5
  213.7 0.0 copy-start.7
  213.7 0.0 copy-start.15
  213.8 1.3 fusion.12
  215.1 0.2 copy-done.11
  215.4 0.3 copy-done.13
  215.7 0.2 copy-done.15
  215.9 0.2 copy-done.17
  216.1 0.2 copy-done.19
  216.3 0.2 copy-done.21
  216.5 17.4 %fusion.4 = bf16[80,16,2048]{2,1,0:T(8,128)(2,1)} fusion(bf16[80,16,2048]{2,1,0:T(8,128)(2,1)} %param.25, f32[80,16]{1,0:T(8,128)S(1)} %copy-done.25, f32[80,2048]{1,0:T(8,128)S(1)} %copy-done.7, f32[80,2048]{1,0:T(8,128)S(1)} %copy-done.15, f32[80,16]{1,0:T(8,128)S(1)} %copy-done.27, f32[80,2048]{1,0:T(8,128)S(1)} %copy-done.9, ...), kind=kLoop, calls=%fused_computation.6 | loop fusion | flops 57671680 | bytes 15880512 | tf_op jit(solution)/shard_map/convert_element_type | solution.py:128
  234.0 25.8 %all-to-all-done.1 = bf16[4,128,2048]{2,1,0:T(8,128)(2,1)} async-done(((bf16[4,128,2048]{2,1,0:T(8,128)(2,1)}), bf16[4,128,2048]{2,1,0:T(8,128)(2,1)}, u32[]{:S(2)}, u32[]{:S(2)}) %all-to-all-start.1) | async-done | bytes 2097184 | tf_op jit(solution)/shard_map/all_to_all | solution.py:133
  259.7 3.3 %convolution_convert_fusion.4 = bf16[256,2048]{1,0:T(8,128)(2,1)} fusion(bf16[512,2048]{1,0:T(8,128)(2,1)} %bitcast.20, s32[512]{0:T(512)S(1)} %copy-done.36, s32[256]{0:T(256)S(1)} %copy-done.38), kind=kOutput, calls=%fused_computation.29 | convolution fusion | flops 537526272 | bytes 3148800 | tf_op jit(solution)/shard_map/dot_general | solution.py:14
  (89 shorter events, 0.2 us)
Async XLA Ops:
  7.2 127.6 %copy-start = (bf16[2048,544]{0,1:T(8,128)(2,1)S(1)}, bf16[2048,544]{0,1:T(8,128)(2,1)}, u32[]{:S(2)}) copy-start(bf16[2048,544]{0,1:T(8,128)(2,1)} %param.19) | copy-start | bytes 6684676
  11.2 3.4 %copy-start.37 = (s32[256]{0:T(256)}, s32[256]{0:T(256)S(1)}, u32[]{:S(2)}) copy-start(s32[256]{0:T(256)S(1)} %add.226) | copy-start | bytes 3076
  11.3 59.0 %copy-start.35 = (s32[512]{0:T(512)}, s32[512]{0:T(512)S(1)}, u32[]{:S(2)}) copy-start(s32[512]{0:T(512)S(1)} %add.230) | copy-start | bytes 6148
  14.6 55.7 %all-to-all-start = ((bf16[4,128,2048]{2,1,0:T(8,128)(2,1)}), bf16[4,128,2048]{2,1,0:T(8,128)(2,1)}, u32[]{:S(2)}, u32[]{:S(2)}) async-start(bf16[4,128,2048]{2,1,0:T(8,128)(2,1)} %bitcast.53), calls=%async_computation | async-start | bytes 4194304 | tf_op jit(solution)/shard_map/all_to_all | solution.py:76
  20.9 92.6 %all-gather.3.cloned.1.call-start = ((), (), s32[]{:S(2)}) async-start(), calls=%async_computation.2 | async-start | bytes 6553600 | tf_op jit(solution)/shard_map/all_gather | solution.py:80
  70.2 3.6 %copy-start.45 = (s32[320]{0:T(512)}, s32[320]{0:T(512)S(1)}, u32[]{:S(2)}) copy-start(s32[320]{0:T(512)S(1)} %select_n.95) | copy-start | bytes 3844
  70.3 4.4 %copy-start.34 = (f32[4,2048]{1,0:T(4,128)S(1)}, f32[4,2048]{1,0:T(4,128)}, u32[]{:S(2)}) copy-start(f32[4,2048]{1,0:T(4,128)} %param.17) | copy-start | bytes 98308
  73.8 98.1 %all-reduce.3.cloned.1.call-start = ((), (), s32[]{:S(2)}) async-start(), calls=%async_computation.3 | async-start | bytes 1638400 | tf_op jit(solution)/shard_map/psum | solution.py:102
  113.5 18.5 %copy-start.4 = (bf16[80,3,2048]{2,0,1:T(8,128)(2,1)S(1)}, bf16[80,3,2048]{2,0,1:T(8,128)(2,1)}, u32[]{:S(2)}) copy-start(bf16[80,3,2048]{2,0,1:T(8,128)(2,1)} %param.26) | copy-start | bytes 2949124
  113.5 18.5 %copy-start.32 = (f32[1,2048]{1,0:T(1,128)S(1)}, f32[1,2048]{1,0:T(1,128)}, u32[]{:S(2)}) copy-start(f32[1,2048]{1,0:T(1,128)} %get-tuple-element.35) | copy-start | bytes 24580
  113.5 18.5 %copy-start.33 = (f32[1,2048]{1,0:T(1,128)S(1)}, f32[1,2048]{1,0:T(1,128)}, u32[]{:S(2)}) copy-start(f32[1,2048]{1,0:T(1,128)} %get-tuple-element.36) | copy-start | bytes 24580
  113.5 18.6 %copy-start.39 = (f32[2048]{0:T(1024)S(1)}, f32[2048]{0:T(1024)}, u32[]{:S(2)}) copy-start(f32[2048]{0:T(1024)} %param.18) | copy-start | bytes 24580
  133.7 1.1 copy-start.2
  134.8 38.4 %copy-start.47 = (f32[2048]{0:T(1024)S(1)}, f32[2048]{0:T(1024)}, u32[]{:S(2)}) copy-start(f32[2048]{0:T(1024)} %param.22) | copy-start | bytes 24580
  134.8 38.4 %copy-start.48 = (f32[512]{0:T(512)S(1)}, f32[512]{0:T(512)}, u32[]{:S(2)}) copy-start(f32[512]{0:T(512)} %param.20) | copy-start | bytes 6148
  137.9 41.5 %copy-start.22 = (f32[16,2048]{1,0:T(8,128)}, f32[16,2048]{1,0:T(8,128)S(1)}, u32[]{:S(2)}) copy-start(f32[16,2048]{1,0:T(8,128)S(1)} %exponential_negate_fusion) | copy-start | bytes 393220
  173.2 3.9 %copy-start.3 = (bf16[4,80,2048]{2,1,0:T(8,128)(2,1)S(1)}, bf16[4,80,2048]{2,1,0:T(8,128)(2,1)}, u32[]{:S(2)}) copy-start(bf16[4,80,2048]{2,1,0:T(8,128)(2,1)} %copy-done.2) | copy-start | bytes 3932164
  177.8 26.1 %copy-start.6 = (f32[80,2048]{1,0:T(8,128)}, f32[80,2048]{1,0:T(8,128)S(1)}, u32[]{:S(2)}) copy-start(f32[80,2048]{1,0:T(8,128)S(1)} %get-tuple-element.11) | copy-start | bytes 1966084
  177.8 26.1 %copy-start.8 = (f32[80,2048]{1,0:T(8,128)}, f32[80,2048]{1,0:T(8,128)S(1)}, u32[]{:S(2)}) copy-start(f32[80,2048]{1,0:T(8,128)S(1)} %get-tuple-element.12) | copy-start | bytes 1966084
  177.8 26.1 %copy-start.10 = (f32[80,2048]{1,0:T(8,128)}, f32[80,2048]{1,0:T(8,128)S(1)}, u32[]{:S(2)}) copy-start(f32[80,2048]{1,0:T(8,128)S(1)} %get-tuple-element.13) | copy-start | bytes 1966084
  177.8 26.1 %copy-start.12 = (f32[80,2048]{1,0:T(8,128)}, f32[80,2048]{1,0:T(8,128)S(1)}, u32[]{:S(2)}) copy-start(f32[80,2048]{1,0:T(8,128)S(1)} %get-tuple-element.14) | copy-start | bytes 1966084
  177.8 26.1 %copy-start.14 = (f32[80,2048]{1,0:T(8,128)}, f32[80,2048]{1,0:T(8,128)S(1)}, u32[]{:S(2)}) copy-start(f32[80,2048]{1,0:T(8,128)S(1)} %get-tuple-element.15) | copy-start | bytes 1966084
  177.9 26.1 %copy-start.16 = (f32[80,2048]{1,0:T(8,128)}, f32[80,2048]{1,0:T(8,128)S(1)}, u32[]{:S(2)}) copy-start(f32[80,2048]{1,0:T(8,128)S(1)} %get-tuple-element.16) | copy-start | bytes 1966084
  177.9 26.1 %copy-start.18 = (f32[80,2048]{1,0:T(8,128)}, f32[80,2048]{1,0:T(8,128)S(1)}, u32[]{:S(2)}) copy-start(f32[80,2048]{1,0:T(8,128)S(1)} %get-tuple-element.17) | copy-start | bytes 1966084
  177.9 26.1 %copy-start.20 = (f32[80,2048]{1,0:T(8,128)}, f32[80,2048]{1,0:T(8,128)S(1)}, u32[]{:S(2)}) copy-start(f32[80,2048]{1,0:T(8,128)S(1)} %get-tuple-element.18) | copy-start | bytes 1966084
  179.3 24.6 %copy-start.24 = (f32[80,16]{1,0:T(8,128)}, f32[80,16]{1,0:T(8,128)S(1)}, u32[]{:S(2)}) copy-start(f32[80,16]{1,0:T(8,128)S(1)} %get-tuple-element.26) | copy-start | bytes 15364
  179.3 24.6 %copy-start.26 = (f32[80,16]{1,0:T(8,128)}, f32[80,16]{1,0:T(8,128)S(1)}, u32[]{:S(2)}) copy-start(f32[80,16]{1,0:T(8,128)S(1)} %get-tuple-element.28) | copy-start | bytes 15364
  179.3 24.6 %copy-start.28 = (f32[80,16]{1,0:T(8,128)}, f32[80,16]{1,0:T(8,128)S(1)}, u32[]{:S(2)}) copy-start(f32[80,16]{1,0:T(8,128)S(1)} %get-tuple-element.30) | copy-start | bytes 15364
  179.4 24.6 %copy-start.30 = (f32[80,16]{1,0:T(8,128)}, f32[80,16]{1,0:T(8,128)S(1)}, u32[]{:S(2)}) copy-start(f32[80,16]{1,0:T(8,128)S(1)} %get-tuple-element.32) | copy-start | bytes 15364
  179.4 24.6 %copy-start.40 = (f32[2048]{0:T(1024)S(1)}, f32[2048]{0:T(1024)}, u32[]{:S(2)}) copy-start(f32[2048]{0:T(1024)} %param.24) | copy-start | bytes 24580
  204.5 0.7 copy-start.36
  204.5 0.7 copy-start.46
  207.8 51.9 %all-to-all-start.1 = ((bf16[4,128,2048]{2,1,0:T(8,128)(2,1)}), bf16[4,128,2048]{2,1,0:T(8,128)(2,1)}, u32[]{:S(2)}, u32[]{:S(2)}) async-start(bf16[4,128,2048]{2,1,0:T(8,128)(2,1)} %bitcast.19), calls=%async_computation.1 | async-start | bytes 4194304 | tf_op jit(solution)/shard_map/all_to_all | solution.py:133
  212.5 1.2 copy-start.5
  212.5 1.2 copy-start.41
  212.5 1.2 copy-start.42
  212.5 1.2 copy-start.43
  212.5 1.2 copy-start.44
  212.5 2.6 copy-start.23
  212.5 2.6 copy-start.25
  212.5 2.6 copy-start.27
  212.5 2.6 copy-start.29
  212.5 2.6 copy-start.31
  213.7 1.5 copy-start.7
  213.7 1.5 copy-start.9
  213.7 1.7 copy-start.11
  213.7 2.0 copy-start.13
  213.7 2.2 copy-start.15
  213.7 2.4 copy-start.17
  213.7 2.6 copy-start.19
  213.7 2.8 %copy-start.21 = (f32[80,2048]{1,0:T(8,128)S(1)}, f32[80,2048]{1,0:T(8,128)}, u32[]{:S(2)}) copy-start(f32[80,2048]{1,0:T(8,128)} %copy-done.20) | copy-start | bytes 1966084
  216.5 43.2 %copy-start.38 = (s32[256]{0:T(256)S(1)}, s32[256]{0:T(256)}, u32[]{:S(2)}) copy-start(s32[256]{0:T(256)} %copy-done.37) | copy-start | bytes 3076
  216.5 46.5 %copy-start.1 = (bf16[2048,544]{0,1:T(8,128)(2,1)S(1)}, bf16[2048,544]{0,1:T(8,128)(2,1)}, u32[]{:S(2)}) copy-start(bf16[2048,544]{0,1:T(8,128)(2,1)} %param.19) | copy-start | bytes 6684676
Sparse Core Ops, SparseCore 0:
  74.0 39.5 all-gather.2
  137.1 34.8 all-reduce.2

commit v2 on v1

v2 whole, which is shorter than its diff:
```python
import functools
import math

import jax
import jax.numpy as jnp
from jax import lax
from jax.experimental import pallas as pl
from jax.experimental.pallas import tpu as pltpu
from jax.sharding import PartitionSpec as P

epsilon = 1e-06


def routing(cache_owner, cache_slot, accepted, slots_here):
    owner_count = lax.axis_size("dp")
    here = lax.axis_index("dp")
    request_count = cache_owner.shape[0]
    capacity = 2 * request_count // owner_count
    place = cache_owner * slots_here + cache_slot
    everyone = lax.all_gather(place * 8 + accepted, "dp", axis=0, tiled=False)
    earlier = jnp.tril(jnp.ones((request_count, request_count), jnp.int32), -1)
    place_all = everyone // 8
    owner_all = place_all // slots_here
    same = (owner_all[:, :, None] == owner_all[:, None, :]).astype(jnp.int32)
    within_all = jnp.sum(same * earlier[None], axis=2)
    mine = (owner_all == here).reshape(-1)
    slot_all = jnp.where(mine, (place_all - here * slots_here).reshape(-1), -1)
    packed_all = (jnp.arange(owner_count)[:, None] * capacity + within_all).reshape(-1)
    match = slot_all[None, :] == jnp.arange(slots_here)[:, None]
    slot_source = jnp.max(jnp.where(match, packed_all[None, :], -1), axis=1)
    slot_accepted = jnp.max(jnp.where(match, (everyone % 8).reshape(-1)[None, :], 0), axis=1)
    own_same = (cache_owner[:, None] == cache_owner[None, :]).astype(jnp.int32)
    send_row = cache_owner * capacity + jnp.sum(own_same * earlier, axis=1)
    return send_row, slot_source, slot_accepted, capacity


MESH = pl.DeviceIdType.MESH
VMEM_LIMIT = 60 * 1024 * 1024


def match(left, right):
    return (left == right).astype(jnp.bfloat16)


def product(left, right):
    return jnp.dot(left, right, preferred_element_type=jnp.float32)


def project_kernel(
    sizes,
    hidden_ref,
    weight_ref,
    request_ref,
    slot_ref,
    base_col_ref,
    base_row_ref,
    out_ref,
    send,
    recv,
    gath,
    wbuf,
    acc,
    w_sem,
    z_send,
    z_recv,
    x_send,
    x_recv,
    s_send,
    s_recv,
):
    owners, lines, chunks, width, block, columns = sizes
    dp = lax.axis_index("dp")
    tensor = lax.axis_index("tensor")
    line = tensor // 2
    core = tensor % 2
    depth = width * chunks

    def origin(step):
        return ((line + lines - step // 2) % lines) * 2 + (core + step) % 2

    weights = []
    for k in range(chunks):
        for g in range(2 * lines):
            first = pl.multiple_of(origin(g) * depth + k * width, width)
            copy = pltpu.make_async_copy(
                weight_ref.at[pl.ds(first, width)], wbuf.at[k, g], w_sem.at[k, g]
            )
            copy.start()
            weights.append(copy)

    barrier = pltpu.get_barrier_semaphore()
    sibling = line * 2 + 1 - core
    pl.semaphore_signal(barrier, inc=1, device_id={"tensor": sibling}, device_id_type=MESH)
    for j in range(1, owners):
        pl.semaphore_signal(
            barrier, inc=1, device_id={"dp": (dp + j) % owners}, device_id_type=MESH
        )
    for j in range(1, lines):
        pl.semaphore_signal(
            barrier,
            inc=1,
            device_id={"tensor": ((line + j) % lines) * 2 + core},
            device_id_type=MESH,
        )
    pl.semaphore_wait(barrier, owners + lines - 1)

    across = {}
    for k in range(chunks):
        part = pl.ds(k * width, width)
        for j in list(range(1, owners)) + [0]:
            target = (dp + j) % owners
            pick = match(base_col_ref[...] + target * block, request_ref[...])
            rows = product(pick, hidden_ref[:, part]).astype(jnp.bfloat16)
            if j == 0:
                recv[k, 0] = rows
            else:
                send[k, j] = rows
                copy = pltpu.make_async_remote_copy(
                    src_ref=send.at[k, j],
                    dst_ref=recv.at[k, j],
                    send_sem=z_send.at[k, j],
                    recv_sem=z_recv.at[k, j],
                    device_id={"dp": target},
                    device_id_type=MESH,
                )
                copy.start()
                across[k, j] = copy

    strip = min(512, columns)

    def multiply(k, g):
        weights[k * 2 * lines + g].wait()

        def body(c, _):
            at = pl.ds(pl.multiple_of(c * strip, strip), strip)
            value = product(gath[k, g], wbuf[k, g, :, at])
            if k == 0 and g == 0:
                acc[:, at] = value
            else:
                acc[:, at] += value
            return 0

        lax.fori_loop(0, columns // strip, body, 0)

    sideways, shared = {}, {}

    def share(k, g):
        copy = pltpu.make_async_remote_copy(
            src_ref=gath.at[k, g],
            dst_ref=gath.at[k, g + 1],
            send_sem=s_send.at[k, g],
            recv_sem=s_recv.at[k, g],
            device_id={"tensor": sibling},
            device_id_type=MESH,
        )
        copy.start()
        shared[k, g] = copy

    def first(k):
        total = None
        for j in range(owners):
            if j:
                across[k, j].wait_recv()
            source = (dp + owners - j) % owners
            pick = match(slot_ref[...], base_row_ref[...] + source * block)
            value = product(pick, recv[k, j])
            total = value if total is None else total + value
        gath[k, 0] = total.astype(jnp.bfloat16)
        for j in range(1, lines):
            copy = pltpu.make_async_remote_copy(
                src_ref=gath.at[k, 0],
                dst_ref=gath.at[k, 2 * j],
                send_sem=x_send.at[k, j],
                recv_sem=x_recv.at[k, j],
                device_id={"tensor": ((line + j) % lines) * 2 + core},
                device_id_type=MESH,
            )
            copy.start()
            sideways[k, j] = copy
        share(k, 0)
        multiply(k, 0)

    def second(k):
        for j in range(1, lines):
            sideways[k, j].wait_recv()
            share(k, 2 * j)
        shared[k, 0].wait_recv()
        multiply(k, 1)
        for j in range(1, lines):
            multiply(k, 2 * j)

    def third(k):
        for j in range(1, lines):
            shared[k, 2 * j].wait_recv()
            multiply(k, 2 * j + 1)

    for step in range(chunks + 2):
        if step < chunks:
            first(step)
        if 1 <= step <= chunks:
            second(step - 1)
        if step >= 2:
            third(step - 2)
    out_ref[...] = acc[...].astype(jnp.bfloat16)
    for copy in list(across.values()) + list(sideways.values()) + list(shared.values()):
        copy.wait_send()


def project(hidden, weight, request_code, slot_code, base, owners, lines, block):
    rows, depth = hidden.shape
    columns = weight.shape[1]
    placed = slot_code.shape[0]
    chunks = 4
    width = depth // chunks
    groups = 2 * lines
    sizes = (owners, lines, chunks, width, block, columns)
    vmem = pl.BlockSpec(memory_space=pltpu.VMEM)
    dma = pltpu.SemaphoreType.DMA
    return pl.pallas_call(
        functools.partial(project_kernel, sizes),
        out_shape=jax.ShapeDtypeStruct((placed, columns), jnp.bfloat16),
        in_specs=[vmem, pl.BlockSpec(memory_space=pl.ANY)] + [vmem] * 4,
        out_specs=vmem,
        scratch_shapes=[
            pltpu.VMEM((chunks, owners, block, width), jnp.bfloat16),
            pltpu.VMEM((chunks, owners, block, width), jnp.bfloat16),
            pltpu.VMEM((chunks, groups, placed, width), jnp.bfloat16),
            pltpu.VMEM((chunks, groups, width, columns), jnp.bfloat16),
            pltpu.VMEM((placed, columns), jnp.float32),
            dma((chunks, groups)),
            dma((chunks, owners)),
            dma((chunks, owners)),
            dma((chunks, lines)),
            dma((chunks, lines)),
            dma((chunks, groups)),
            dma((chunks, groups)),
        ],
        compiler_params=pltpu.CompilerParams(
            collective_id=0, has_side_effects=True, vmem_limit_bytes=VMEM_LIMIT
        ),
        cost_estimate=pl.CostEstimate(
            flops=2 * placed * depth * groups * columns,
            bytes_accessed=2 * depth * groups * columns,
            transcendentals=0,
        ),
    )(hidden, weight, request_code[None, :], slot_code[:, None], base[:, None], base[None, :])


def return_kernel(
    sizes,
    rows_ref,
    request_ref,
    slot_ref,
    base_col_ref,
    base_row_ref,
    out_ref,
    send,
    recv,
    z_send,
    z_recv,
):
    owners, chunks, width, block = sizes
    dp = lax.axis_index("dp")
    barrier = pltpu.get_barrier_semaphore()
    for j in range(1, owners):
        pl.semaphore_signal(
            barrier, inc=1, device_id={"dp": (dp + j) % owners}, device_id_type=MESH
        )
    pl.semaphore_wait(barrier, owners - 1)
    across = {}
    for k in range(chunks):
        part = pl.ds(k * width, width)
        for j in list(range(1, owners)) + [0]:
            target = (dp + j) % owners
            pick = match(base_col_ref[...] + target * block, slot_ref[...])
            rows = product(pick, rows_ref[:, part]).astype(jnp.bfloat16)
            if j == 0:
                recv[k, 0] = rows
            else:
                send[k, j] = rows
                copy = pltpu.make_async_remote_copy(
                    src_ref=send.at[k, j],
                    dst_ref=recv.at[k, j],
                    send_sem=z_send.at[k, j],
                    recv_sem=z_recv.at[k, j],
                    device_id={"dp": target},
                    device_id_type=MESH,
                )
                copy.start()
                across[k, j] = copy
    for k in range(chunks):
        total = None
        for j in range(owners):
            if j:
                across[k, j].wait_recv()
            source = (dp + owners - j) % owners
            pick = match(request_ref[...], base_row_ref[...] + source * block)
            value = product(pick, recv[k, j])
            total = value if total is None else total + value
        out_ref[:, pl.ds(k * width, width)] = total.astype(jnp.bfloat16)
    for copy in across.values():
        copy.wait_send()


def send_back(rows, request_code, slot_code, base, owners, block):
    columns = rows.shape[1]
    chunks = 4
    width = columns // chunks
    vmem = pl.BlockSpec(memory_space=pltpu.VMEM)
    dma = pltpu.SemaphoreType.DMA
    return pl.pallas_call(
        functools.partial(return_kernel, (owners, chunks, width, block)),
        out_shape=jax.ShapeDtypeStruct((request_code.shape[0], columns), jnp.bfloat16),
        in_specs=[vmem] * 5,
        out_specs=vmem,
        scratch_shapes=[
            pltpu.VMEM((chunks, owners, block, width), jnp.bfloat16),
            pltpu.VMEM((chunks, owners, block, width), jnp.bfloat16),
            dma((chunks, owners)),
            dma((chunks, owners)),
        ],
        compiler_params=pltpu.CompilerParams(
            collective_id=1, has_side_effects=True, vmem_limit_bytes=VMEM_LIMIT
        ),
    )(rows, request_code[:, None], slot_code[None, :], base[:, None], base[None, :])


def mix_kernel(
    tokens,
    inputs_ref,
    window_ref,
    taps_ref,
    bias_ref,
    select_ref,
    accepted_ref,
    activated_ref,
    partial_ref,
    rolled_ref,
):
    kept, slots, width = window_ref.shape

    def row(position):
        if position < kept:
            return window_ref[position]
        return inputs_ref[pl.ds((position - kept) * slots, slots), :]

    window = [row(position) for position in range(kept + tokens)]
    wide = [value.astype(jnp.float32) for value in window]
    for t in range(tokens):
        mixed = bias_ref[...] + taps_ref[pl.ds(0, 1), :] * wide[t]
        for tap in range(1, taps_ref.shape[0]):
            mixed = mixed + taps_ref[pl.ds(tap, 1), :] * wide[t + tap]
        activated_ref[pl.ds(t * slots, slots), :] = (mixed * jax.nn.sigmoid(mixed)).astype(
            jnp.bfloat16
        )
    accepted = jnp.broadcast_to(accepted_ref[...], (slots, width))
    for place in range(kept):
        chosen = wide[place]
        for position in range(1, tokens + 1):
            chosen = jnp.where(accepted == position, wide[position + place], chosen)
        rolled_ref[place] = chosen.astype(jnp.bfloat16)
    value = lax.dot_general(
        activated_ref[...],
        select_ref[...],
        (((1,), (1,)), ((), ())),
        preferred_element_type=jnp.float32,
    )

    @pl.when(pl.program_id(0) == 0)
    def _():
        partial_ref[...] = value

    @pl.when(pl.program_id(0) > 0)
    def _():
        partial_ref[...] += value


def mix(inputs, window, kernel_weight, kernel_bias, select_rows, slot_accepted, tokens):
    kept, slots, channels = window.shape
    width = min(512, channels)
    return pl.pallas_call(
        functools.partial(mix_kernel, tokens),
        grid=(channels // width,),
        out_shape=(
            jax.ShapeDtypeStruct(inputs.shape, jnp.bfloat16),
            jax.ShapeDtypeStruct((inputs.shape[0], select_rows.shape[0]), jnp.float32),
            jax.ShapeDtypeStruct(window.shape, jnp.bfloat16),
        ),
        in_specs=[
            pl.BlockSpec((inputs.shape[0], width), lambda i: (0, i)),
            pl.BlockSpec((kept, slots, width), lambda i: (0, 0, i)),
            pl.BlockSpec((kernel_weight.shape[0], width), lambda i: (0, i)),
            pl.BlockSpec((1, width), lambda i: (0, i)),
            pl.BlockSpec((select_rows.shape[0], width), lambda i: (0, i)),
            pl.BlockSpec((slots, 1), lambda i: (0, 0)),
        ],
        out_specs=(
            pl.BlockSpec((inputs.shape[0], width), lambda i: (0, i)),
            pl.BlockSpec((inputs.shape[0], select_rows.shape[0]), lambda i: (0, 0)),
            pl.BlockSpec((kept, slots, width), lambda i: (0, 0, i)),
        ),
        compiler_params=pltpu.CompilerParams(vmem_limit_bytes=VMEM_LIMIT),
    )(inputs, window, kernel_weight, kernel_bias[None, :], select_rows, slot_accepted[:, None])


def recur_kernel(
    tokens,
    accepted_ref,
    projected_ref,
    gain_ref,
    step_weight_ref,
    step_bias_ref,
    decay_ref,
    skip_ref,
    activated_ref,
    state_ref,
    into_ref,
    outof_ref,
    out_ref,
    new_state_ref,
    normed,
    step,
    scaled,
    result,
    rate,
):
    slots, states, width = state_ref.shape

    @pl.when(pl.program_id(0) == 0)
    def _():
        rank = gain_ref.shape[1]
        part = projected_ref[:, pl.ds(0, rank)]
        norm = lax.rsqrt(jnp.mean(part * part, axis=1, keepdims=True) + epsilon)
        normed[...] = (part * norm * gain_ref[...]).astype(jnp.bfloat16)

    raw = product(normed[...], step_weight_ref[...]) + step_bias_ref[...]
    size = jnp.maximum(raw, 0.0) + jnp.log1p(jnp.exp(-jnp.abs(raw)))
    step[...] = size
    scaled[...] = size * activated_ref[...].astype(jnp.float32)
    rate[...] = jnp.exp(decay_ref[...]) * (-math.log2(math.e))
    lanes = 128

    tiles = width // lanes
    group = 8

    def body(index, _):
        first = pl.multiple_of((index // tiles) * group, group)
        at = pl.ds(pl.multiple_of((index % tiles) * lanes, lanes), lanes)
        fading = rate[:, at]
        sizes, inputs = [], []
        for t in range(tokens):
            rows = pl.ds(pl.multiple_of(t * slots + first, group), group)
            sizes.append(step[rows, at])
            inputs.append(scaled[rows, at])
        sums = [[] for _ in range(tokens)]
        for i in range(group):
            taken = accepted_ref[first + i]
            carried = state_ref[first + i, :, at].astype(jnp.float32)
            chosen = carried
            for t in range(tokens):
                row = t * slots + first + i
                fade = jnp.exp2(sizes[t][i : i + 1] * fading)
                carried = fade * carried + inputs[t][i : i + 1] * into_ref[row]
                sums[t].append(jnp.sum(outof_ref[row] * carried, axis=0, keepdims=True))
                chosen = jnp.where(taken == t + 1, carried, chosen)
            new_state_ref[first + i, :, at] = chosen.astype(jnp.bfloat16)
        for t in range(tokens):
            rows = pl.ds(pl.multiple_of(t * slots + first, group), group)
            result[rows, at] = jnp.concatenate(sums[t], axis=0)
        return 0

    lax.fori_loop(0, slots // group * tiles, body, 0)
    out_ref[...] = (
        result[...] + skip_ref[...] * activated_ref[...].astype(jnp.float32)
    ).astype(jnp.bfloat16)


def recur(
    slot_accepted,
    projected,
    step_gain,
    step_weight,
    step_bias,
    decay_log,
    skip_gain,
    activated,
    state_cache,
    tokens,
):
    slots, states, channels = state_cache.shape
    rows = activated.shape[0]
    rank = step_gain.shape[0]
    width = min(512, channels)
    lanes = 128
    into = jnp.broadcast_to(
        projected[:, rank : rank + states, None], (rows, states, lanes)
    )
    outof = jnp.broadcast_to(projected[:, rank + states :, None], (rows, states, lanes))
    whole = lambda shape: pl.BlockSpec(shape, lambda i, accepted: (0,) * len(shape))
    strip = lambda count: pl.BlockSpec((count, width), lambda i, accepted: (0, i))
    return pl.pallas_call(
        functools.partial(recur_kernel, tokens),
        out_shape=(
            jax.ShapeDtypeStruct((rows, channels), jnp.bfloat16),
            jax.ShapeDtypeStruct(state_cache.shape, jnp.bfloat16),
        ),
        grid_spec=pltpu.PrefetchScalarGridSpec(
            num_scalar_prefetch=1,
            grid=(channels // width,),
            in_specs=[
                whole(projected.shape),
                whole((1, rank)),
                strip(rank),
                strip(1),
                strip(states),
                strip(1),
                strip(rows),
                pl.BlockSpec((slots, states, width), lambda i, accepted: (0, 0, i)),
                whole((rows, states, lanes)),
                whole((rows, states, lanes)),
            ],
            out_specs=(
                strip(rows),
                pl.BlockSpec((slots, states, width), lambda i, accepted: (0, 0, i)),
            ),
            scratch_shapes=[
                pltpu.VMEM((rows, rank), jnp.bfloat16),
                pltpu.VMEM((rows, width), jnp.float32),
                pltpu.VMEM((rows, width), jnp.float32),
                pltpu.VMEM((rows, width), jnp.float32),
                pltpu.VMEM((states, width), jnp.float32),
            ],
        ),
        compiler_params=pltpu.CompilerParams(vmem_limit_bytes=VMEM_LIMIT),
    )(
        slot_accepted,
        projected,
        step_gain[None, :],
        step_weight,
        step_bias[None, :],
        decay_log,
        skip_gain[None, :],
        activated,
        state_cache,
        into,
        outof,
    )


def on_device(
    hidden_input,
    input_weight,
    kernel_weight,
    kernel_bias,
    select_weight,
    step_gain,
    step_weight,
    step_bias,
    decay_log,
    skip_gain,
    state_cache,
    window_cache,
    cache_owner,
    cache_slot,
    accepted,
):
    owner_count = lax.axis_size("dp")
    slots, states, channels = state_cache.shape
    kept = window_cache.shape[1]
    request_count = cache_owner.shape[0]
    tokens = hidden_input.shape[0] // request_count
    send_row, slot_source, slot_accepted, capacity = routing(
        cache_owner, cache_slot, accepted, slots
    )
    lines = lax.axis_size("tensor") // 2
    block = tokens * capacity
    token_axis = jnp.arange(tokens, dtype=jnp.int32)
    request_code = (send_row[:, None] * tokens + token_axis[None, :]).reshape(-1)
    base = (
        jnp.arange(capacity, dtype=jnp.int32)[None, :] * tokens + token_axis[:, None]
    ).reshape(-1)
    slot_code = jnp.where(
        slot_source[None, :] >= 0, slot_source[None, :] * tokens + token_axis[:, None], -1
    ).reshape(-1)
    inputs = project(
        hidden_input, input_weight, request_code, slot_code, base, owner_count, lines, block
    )
    activated, partial_value, rolled = mix(
        inputs,
        jnp.transpose(window_cache, (1, 0, 2)),
        kernel_weight,
        kernel_bias,
        select_weight.T,
        slot_accepted,
        tokens,
    )
    projected = lax.psum(partial_value, "tensor")
    outputs, new_state_cache = recur(
        slot_accepted,
        projected,
        step_gain,
        step_weight,
        step_bias,
        decay_log,
        skip_gain,
        activated,
        state_cache,
        tokens,
    )
    mamba_output = send_back(outputs, request_code, slot_code, base, owner_count, block)
    return mamba_output, new_state_cache, jnp.transpose(rolled, (1, 0, 2))


def solution(mesh):
    in_specs = (
        P(("groups", "dp"), "tensor"),
        P(None, "tensor"),
        P(None, "tensor"),
        P("tensor"),
        P("tensor", None),
        P(),
        P(None, "tensor"),
        P("tensor"),
        P(None, "tensor"),
        P("tensor"),
        P(("groups", "dp"), None, "tensor"),
        P(("groups", "dp"), None, "tensor"),
        P(("groups", "dp")),
        P(("groups", "dp")),
        P(("groups", "dp")),
    )
    out_specs = (
        P(("groups", "dp"), "tensor"),
        P(("groups", "dp"), None, "tensor"),
        P(("groups", "dp"), None, "tensor"),
    )
    return jax.shard_map(
        on_device, mesh=mesh, in_specs=in_specs, out_specs=out_specs, check_vma=False
    )
```

time: 271 us -> 227 us (0.84)
  Pallas kernels: 0 us -> 148 us
  waiting for transfers between devices: 98.1 us -> 37.3 us
  other arithmetic: 51.1 us -> 2.24 us
  blocking collectives: 48.4 us -> 9.89 us
  matrix products: 37.3 us -> 0 us
  starting transfers between devices: 11.2 us -> 0.04 us
  local copies, waits for them, and re-layouts: 8.27 us -> 13.8 us
    pallas_call x0 -> x4, Pallas kernels: none -> 148 us  [the longest x1 63.5 us: project(): pl.pallas_call(functools.partial(project_kernel, sizes), out_shape=jax.Sh...]
    unnamed x1, blocking collectives: 48.4 us -> 9.89 us
    all_gather x1 -> x0, waiting for transfers between devices: 38.3 us -> none  [on_device(): gathered = lax.all_gather(placed, 'tensor', axis=1, tiled=True)]
    dot_general x7 -> x0, matrix products: 37.3 us -> none  [the longest x1 18.5 us: on_device(): jnp.dot(gathered, input_weight, preferred_element_type=jnp.float32)]
    all_to_all x2 -> x0, waiting for transfers between devices: 25.8 us -> none  [the longest x1 25.8 us: on_device(): lax.all_to_all(returning, 'dp', split_axis=0, concat_axis=0, tiled=True)]
    reduce_sum x2 -> x1, other arithmetic: 25.7 us -> 0.92 us  [routing(): send_row = cache_owner * capacity + jnp.sum(own_same * earlier, axis=1)]
    convert_element_type x2 -> x0, other arithmetic: 19 us -> none  [the longest x1 17.4 us: on_device(): new_state_cache = kept_state.astype(jnp.bfloat16)]
    all_to_all x2 -> x0, starting transfers between devices: 11 us -> none  [the longest x1 6.32 us: on_device(): lax.all_to_all(outgoing, 'dp', split_axis=0, concat_axis=0, tiled=True)]
  transfers between devices with their start and end apart: 4 -> 1, of which waited for: 3 -> 1; matrix products, arithmetic and copies ran while one was open for 8% -> 1% of each run, Pallas kernels for 0% -> 0%
where the time goes in v2:
time: 227 us; the launch traced here: 226 us
  Pallas kernels  148 us (65%)
  waiting for transfers between devices  37.3 us (16%)
  between operations  14.8 us (7%)
  local copies, waits for them, and re-layouts  13.8 us (6%)
  blocking collectives  9.89 us (4%)
    pallas_call x1, Pallas kernels, project(): pl.pallas_call(functools.partial(project_kernel, sizes), out_shape=jax.Sh...  63.5 us
    pallas_call x1, Pallas kernels, send_back(): pl.pallas_call(functools.partial(return_kernel, (owners, chunks, width, b...  48.9 us
    psum x1, waiting for transfers between devices, on_device(): projected = lax.psum(partial_value, 'tensor')  37.3 us
    pallas_call x1, Pallas kernels, recur(): pl.pallas_call(functools.partial(recur_kernel, tokens), out_shape=(jax.Sh...  29.3 us
    unnamed x1, blocking collectives  9.89 us
    pallas_call x1, Pallas kernels, mix(): pl.pallas_call(functools.partial(mix_kernel, tokens), grid=(channels // w...  6.17 us
  transfers between devices with their start and end apart: 1, of which 1 were waited for; matrix products, arithmetic and copies ran while one was open for 1% of the time, Pallas kernels for 0%

profile of v2, /device:TPU:0, one launch (start us, length us, event | category | flops | bytes accessed | tf_op | source)
XLA Modules:
  0.0 225.9 jit_solution(9307582178901492158)
XLA Ops:
  7.2 0.0 all-reduce.3.cloned.1.call-start
  7.2 0.9 select_reduce_fusion.3
  8.2 1.2 dynamic-slice
  10.1 0.8 add_multiply_fusion
  10.9 9.9 %all-reduce = s32[256]{0:T(256)S(1)} all-reduce(s32[256]{0:T(256)S(1)} %get-tuple-element.21), channel_id=2, replica_groups=mesh['groups'=2,'tensor'=4,'dp'=4] {'dp'}, use_global_device_ids=true, to_apply=%add | all-reduce | flops 256 | bytes 2048
  20.7 0.1 reshape.232
  20.8 0.2 select_reduce_fusion
  21.1 0.1 broadcast_add_fusion
  21.1 0.1 add.174
  21.2 0.1 broadcast_in_dim.85
  21.3 0.1 select_n.70
  21.4 0.1 select_reduce_fusion.1
  21.5 0.0 copy-start
  21.6 0.7 add.186.base_col_ref
  22.3 0.6 add.182.base_row_ref
  22.9 0.8 select_n.78.slot_ref
  23.7 0.1 iota_add_fusion
  23.8 0.7 add.171.request_ref
  24.4 0.7 copy.28.accepted_ref
  25.2 63.5 %shard_map.166.inputs_ref = bf16[320,2048]{1,0:T(8,128)(2,1)} custom-call(bf16[256,2048]{1,0:T(8,128)(2,1)} %hidden_ref.1, bf16[8192,2048]{1,0:T(8,128)(2,1)} %weight_ref.1, s32[1,256]{1,0:T(1,128)} %add.171.request_ref, s32[320,1]{1,0:T(8,128)} %select_n.78.slot_ref, s32[128,1]{1,0:T(8,128)} %add.186.base_col_ref, s32[1,128]{1,0:T(1,128)} %add.182.base_row_ref), custom_call_target="tpu_custom_call" | custom-call | flops 10737418240 | bytes 33554432 | tf_op jit(solution)/shard_map/pallas_call | solution.py:219
  88.7 0.0 copy-done
  88.7 6.2 %shard_map.167 = (bf16[320,2048]{1,0:T(8,128)(2,1)}, f32[320,544]{1,0:T(8,128)}, bf16[3,80,2048]{2,1,0:T(8,128)(2,1)}) custom-call(bf16[320,2048]{1,0:T(8,128)(2,1)} %shard_map.166.inputs_ref, bf16[3,80,2048]{2,1,0:T(8,128)(2,1)} %bitcast.10, f32[4,2048]{1,0:T(4,128)} %taps_ref.1, f32[1,2048]{1,0:T(1,128)} %bitcast.11, bf16[544,2048]{1,0:T(8,128)(2,1)} %bitcast.9, ...), custom_call_target="tpu_custom_call" | custom-call | tf_op jit(solution)/shard_map/pallas_call | solution.py:381
  94.9 0.0 all-reduce.3.cloned.1.call-update
  94.9 0.7 select_n.77.slot_ref
  95.6 0.7 add.187.request_ref
  96.3 37.3 %all-reduce.3.cloned.1.call-done.projected_ref = f32[320,544]{1,0:T(8,128)} async-done(((f32[320,544]{1,0:T(8,128)}), f32[320,544]{1,0:T(8,128)}) %all-reduce.3.cloned.1.call-update) | async-done | bytes 696336 | tf_op jit(solution)/shard_map/psum | solution.py:597
  133.6 1.1 fusion.3
  134.7 2.0 broadcast_in_dim.100.outof_ref
  136.6 1.9 broadcast_in_dim.99.into_ref
  138.5 29.3 %shard_map.168 = (bf16[320,2048]{1,0:T(8,128)(2,1)}, bf16[80,16,2048]{2,1,0:T(8,128)(2,1)}) custom-call(s32[80]{0:T(128)} %copy-done, f32[320,544]{1,0:T(8,128)} %all-reduce.3.cloned.1.call-done.projected_ref, f32[1,512]{1,0:T(1,128)} %bitcast.15, bf16[512,2048]{1,0:T(8,128)(2,1)} %step_weight_ref.1, f32[1,2048]{1,0:T(1,128)} %bitcast.12, ...), custom_call_target="tpu_custom_call" | custom-call | tf_op jit(solution)/shard_map/pallas_call | solution.py:501
  167.8 48.9 %shard_map.169 = bf16[256,2048]{1,0:T(8,128)(2,1)} custom-call(bf16[320,2048]{1,0:T(8,128)(2,1)} %get-tuple-element.10.rows_ref, s32[256,1]{1,0:T(8,128)} %add.187.request_ref, s32[1,320]{1,0:T(1,128)} %select_n.77.slot_ref, s32[128,1]{1,0:T(8,128)} %add.186.base_col_ref, s32[1,128]{1,0:T(1,128)} %add.182.base_row_ref), custom_call_target="tpu_custom_call" | custom-call | tf_op jit(solution)/shard_map/pallas_call | solution.py:311
  216.8 2.3 %copy.34 = bf16[256,2048]{1,0:T(8,128)(2,1)} copy(bf16[256,2048]{1,0:T(8,128)(2,1)} %shard_map.169) | data formatting | bytes 2097152
  (9 shorter events, 0.1 us)
Async XLA Ops:
  7.2 126.4 %all-reduce.3.cloned.1.call-start = ((), (), s32[]{:S(2)}) async-start(), calls=%async_computation | async-start | bytes 1638400 | tf_op jit(solution)/shard_map/psum | solution.py:597
  21.5 67.2 %copy-start = (s32[80]{0:T(128)}, s32[80]{0:T(128)S(1)}, u32[]{:S(2)}) copy-start(s32[80]{0:T(128)S(1)} %get-tuple-element.14.accepted_ref) | copy-start | bytes 964
Sparse Core Ops, SparseCore 0:
  95.0 38.5 all-reduce.2

commit v3 on v2

--- a/solution.py
+++ b/solution.py
@@ -403,6 +403,107 @@
     )(inputs, window, kernel_weight, kernel_bias[None, :], select_rows, slot_accepted[:, None])
 
 
+def total_kernel(
+    sizes, mine_ref, out_ref, pair, held, lines_in, p_send, p_recv, x_send, x_recv, s_send, s_recv
+):
+    lines, pieces, piece = sizes
+    tensor = lax.axis_index("tensor")
+    line = tensor // 2
+    core = tensor % 2
+    sibling = line * 2 + 1 - core
+    half = pieces * piece
+    barrier = pltpu.get_barrier_semaphore()
+    pl.semaphore_signal(barrier, inc=1, device_id={"tensor": sibling}, device_id_type=MESH)
+    for j in range(1, lines):
+        pl.semaphore_signal(
+            barrier,
+            inc=1,
+            device_id={"tensor": ((line + j) % lines) * 2 + core},
+            device_id_type=MESH,
+        )
+    pl.semaphore_wait(barrier, lines)
+
+    def send(source, target, sends, arrives, device):
+        copy = pltpu.make_async_remote_copy(
+            src_ref=source,
+            dst_ref=target,
+            send_sem=sends,
+            recv_sem=arrives,
+            device_id={"tensor": device},
+            device_id_type=MESH,
+        )
+        copy.start()
+        return copy
+
+    def rows(owner, p):
+        return pl.ds(pl.multiple_of(owner * half + p * piece, 8), piece)
+
+    paired = [
+        send(mine_ref.at[rows(1 - core, p)], pair.at[p], p_send.at[p], p_recv.at[p], sibling)
+        for p in range(pieces)
+    ]
+    crossed = {}
+    for p in range(pieces):
+        paired[p].wait_recv()
+        held[p] = mine_ref[rows(core, p), :] + pair[p]
+        for j in range(1, lines):
+            crossed[p, j] = send(
+                held.at[p],
+                lines_in.at[p, j],
+                x_send.at[p, j],
+                x_recv.at[p, j],
+                ((line + j) % lines) * 2 + core,
+            )
+    final = []
+    for p in range(pieces):
+        value = held[p]
+        for j in range(1, lines):
+            crossed[p, j].wait_recv()
+            value = value + lines_in[p, j]
+        out_ref[rows(core, p), :] = value
+        final.append(
+            send(
+                out_ref.at[rows(core, p)],
+                out_ref.at[rows(core, p)],
+                s_send.at[p],
+                s_recv.at[p],
+                sibling,
+            )
+        )
+    for copy in final:
+        copy.wait_recv()
+    for copy in paired + list(crossed.values()) + final:
+        copy.wait_send()
+
+
+def total(partial_value, lines):
+    rows, columns = partial_value.shape
+    pieces = 4
+    piece = rows // (2 * pieces)
+    vmem = pl.BlockSpec(memory_space=pltpu.VMEM)
+    dma = pltpu.SemaphoreType.DMA
+    return pl.pallas_call(
+        functools.partial(total_kernel, (lines, pieces, piece)),
+        out_shape=jax.ShapeDtypeStruct((rows, columns), jnp.float32),
+        in_specs=[vmem],
+        out_specs=vmem,
+        scratch_shapes=[
+            pltpu.VMEM((pieces, piece, columns), jnp.float32),
+            pltpu.VMEM((pieces, piece, columns), jnp.float32),
+            pltpu.VMEM((pieces, lines, piece, columns), jnp.float32),
+            dma((pieces,)),
+            dma((pieces,)),
+            dma((pieces, lines)),
+            dma((pieces, lines)),
+            dma((pieces,)),
+            dma((pieces,)),
+        ],
+        compiler_params=pltpu.CompilerParams(
+            collective_id=2, has_side_effects=True, vmem_limit_bytes=VMEM_LIMIT
+        ),
+    )(partial_value)
+
+
 def recur_kernel(
     tokens,
     accepted_ref,
@@ -594,7 +695,7 @@
         slot_accepted,
         tokens,
     )
-    projected = lax.psum(partial_value, "tensor")
+    projected = total(partial_value, lines)
     outputs, new_state_cache = recur(
         slot_accepted,
         projected,

time: 227 us -> 196 us (0.86)
  waiting for transfers between devices: 37.3 us -> 0 us
  Pallas kernels: 148 us -> 168 us
  between operations: 14.8 us -> 1.4 us
    psum x1 -> x0, waiting for transfers between devices: 37.3 us -> none  [on_device(): projected = lax.psum(partial_value, 'tensor')]
    pallas_call x0 -> x1, Pallas kernels: none -> 15.4 us  [total(): pl.pallas_call(functools.partial(total_kernel, (lines, pieces, piece)), o...]
    pallas_call x1, Pallas kernels: 48.9 us -> 53.9 us  [send_back(): pl.pallas_call(functools.partial(return_kernel, (owners, chunks, width, b...]
  transfers between devices with their start and end apart: 1 -> 0, of which waited for: 1 -> 0; matrix products, arithmetic and copies ran while one was open for 1% -> 0% of each run, Pallas kernels for 0% -> 0%
where the time goes in v3:
time: 196 us
  Pallas kernels  168 us (86%)
  local copies, waits for them, and re-layouts  13.9 us (7%)
  blocking collectives  9.89 us (5%)
  other arithmetic  2.24 us (1%)
    pallas_call x1, Pallas kernels, project(): pl.pallas_call(functools.partial(project_kernel, sizes), out_shape=jax.Sh...  63.5 us
    pallas_call x1, Pallas kernels, send_back(): pl.pallas_call(functools.partial(return_kernel, (owners, chunks, width, b...  53.9 us
    pallas_call x1, Pallas kernels, recur(): pl.pallas_call(functools.partial(recur_kernel, tokens), out_shape=(jax.Sh...  29.3 us
    pallas_call x1, Pallas kernels, total(): pl.pallas_call(functools.partial(total_kernel, (lines, pieces, piece)), o...  15.4 us
    unnamed x1, blocking collectives  9.89 us
    pallas_call x1, Pallas kernels, mix(): pl.pallas_call(functools.partial(mix_kernel, tokens), grid=(channels // w...  6.15 us

profile of v3, /device:TPU:0, one launch (start us, length us, event | category | flops | bytes accessed | tf_op | source)
XLA Modules:
  0.0 195.6 jit_solution(7763598037120706532)
XLA Ops:
  0.6 0.9 select_reduce_fusion.3
  1.6 1.2 dynamic-slice
  3.5 0.8 add_multiply_fusion
  4.3 9.9 %all-reduce = s32[256]{0:T(256)S(1)} all-reduce(s32[256]{0:T(256)S(1)} %get-tuple-element.21), channel_id=2, replica_groups=mesh['groups'=2,'tensor'=4,'dp'=4] {'dp'}, use_global_device_ids=true, to_apply=%add | all-reduce | flops 256 | bytes 2048
  14.1 0.1 reshape.232
  14.3 0.2 select_reduce_fusion
  14.5 0.1 broadcast_add_fusion
  14.6 0.1 add.172
  14.6 0.1 broadcast_in_dim.85
  14.7 0.1 select_n.70
  14.8 0.1 select_reduce_fusion.1
  14.9 0.0 copy-start
  15.0 0.8 select_n.78.slot_ref
  15.8 0.1 iota_add_fusion
  15.9 0.7 add.169.request_ref
  16.6 0.7 add.184.base_col_ref
  17.3 0.7 add.180.base_row_ref
  17.9 63.5 %shard_map.166.inputs_ref = bf16[320,2048]{1,0:T(8,128)(2,1)} custom-call(bf16[256,2048]{1,0:T(8,128)(2,1)} %hidden_ref.1, bf16[8192,2048]{1,0:T(8,128)(2,1)} %weight_ref.1, s32[1,256]{1,0:T(1,128)} %add.169.request_ref, s32[320,1]{1,0:T(8,128)} %select_n.78.slot_ref, s32[128,1]{1,0:T(8,128)} %add.184.base_col_ref, s32[1,128]{1,0:T(1,128)} %add.180.base_row_ref), custom_call_target="tpu_custom_call" | custom-call | flops 10737418240 | bytes 33554432 | tf_op jit(solution)/shard_map/pallas_call | solution.py:219
  81.5 0.0 copy-done
  81.5 0.7 copy.28.accepted_ref
  82.2 6.1 %shard_map.167 = (bf16[320,2048]{1,0:T(8,128)(2,1)}, f32[320,544]{1,0:T(8,128)}, bf16[3,80,2048]{2,1,0:T(8,128)(2,1)}) custom-call(bf16[320,2048]{1,0:T(8,128)(2,1)} %shard_map.166.inputs_ref, bf16[3,80,2048]{2,1,0:T(8,128)(2,1)} %bitcast.10, f32[4,2048]{1,0:T(4,128)} %taps_ref.1, f32[1,2048]{1,0:T(1,128)} %bitcast.11, bf16[544,2048]{1,0:T(8,128)(2,1)} %bitcast.9, ...), custom_call_target="tpu_custom_call" | custom-call | tf_op jit(solution)/shard_map/pallas_call | solution.py:381
  88.3 15.4 %shard_map.168.projected_ref = f32[320,544]{1,0:T(8,128)} custom-call(f32[320,544]{1,0:T(8,128)} %get-tuple-element.8.mine_ref), custom_call_target="tpu_custom_call" | custom-call | tf_op jit(solution)/shard_map/pallas_call | solution.py:485
  103.7 1.1 fusion.3
  104.8 2.0 broadcast_in_dim.100.outof_ref
  106.8 1.9 broadcast_in_dim.99.into_ref
  108.7 29.3 %shard_map.169 = (bf16[320,2048]{1,0:T(8,128)(2,1)}, bf16[80,16,2048]{2,1,0:T(8,128)(2,1)}) custom-call(s32[80]{0:T(128)} %copy-done, f32[320,544]{1,0:T(8,128)} %shard_map.168.projected_ref, f32[1,512]{1,0:T(1,128)} %bitcast.15, bf16[512,2048]{1,0:T(8,128)(2,1)} %step_weight_ref.1, f32[1,2048]{1,0:T(1,128)} %bitcast.12, f32[16,2048]{1,0:T(8,128)} %decay_ref.1, ...), custom_call_target="tpu_custom_call" | custom-call | tf_op jit(solution)/shard_map/pallas_call | solution.py:602
  138.0 0.7 select_n.77.slot_ref
  138.6 0.7 add.185.request_ref
  139.4 53.9 %shard_map.170 = bf16[256,2048]{1,0:T(8,128)(2,1)} custom-call(bf16[320,2048]{1,0:T(8,128)(2,1)} %get-tuple-element.10.rows_ref, s32[256,1]{1,0:T(8,128)} %add.185.request_ref, s32[1,320]{1,0:T(1,128)} %select_n.77.slot_ref, s32[128,1]{1,0:T(8,128)} %add.184.base_col_ref, s32[1,128]{1,0:T(1,128)} %add.180.base_row_ref), custom_call_target="tpu_custom_call" | custom-call | tf_op jit(solution)/shard_map/pallas_call | solution.py:311
  193.3 2.3 %copy.33 = bf16[256,2048]{1,0:T(8,128)(2,1)} copy(bf16[256,2048]{1,0:T(8,128)(2,1)} %shard_map.170) | data formatting | bytes 2097152
  (9 shorter events, 0.1 us)
Async XLA Ops:
  14.9 66.5 %copy-start = (s32[80]{0:T(128)}, s32[80]{0:T(128)S(1)}, u32[]{:S(2)}) copy-start(s32[80]{0:T(128)S(1)} %get-tuple-element.14.accepted_ref) | copy-start | bytes 964

commit v4 on v3

--- a/solution.py
+++ b/solution.py
@@ -210,7 +210,7 @@
     rows, depth = hidden.shape
     columns = weight.shape[1]
     placed = slot_code.shape[0]
-    chunks = 4
+    chunks = max(1, depth // 256)
     width = depth // chunks
     groups = 2 * lines
     sizes = (owners, lines, chunks, width, block, columns)
@@ -304,7 +304,7 @@
 
 def send_back(rows, request_code, slot_code, base, owners, block):
     columns = rows.shape[1]
-    chunks = 4
+    chunks = max(1, columns // 256)
     width = columns // chunks
     vmem = pl.BlockSpec(memory_space=pltpu.VMEM)
     dma = pltpu.SemaphoreType.DMA

time: 196 us -> 200 us (1.020)
  Pallas kernels: 168 us -> 172 us
    pallas_call x1, Pallas kernels: 63.5 us -> 67.9 us  [project(): pl.pallas_call(functools.partial(project_kernel, sizes), out_shape=jax.Sh...]
where the time goes in v4:
time: 200 us
  Pallas kernels  172 us (86%)
  local copies, waits for them, and re-layouts  13.9 us (7%)
  blocking collectives  9.89 us (5%)
  other arithmetic  2.24 us (1%)
    pallas_call x1, Pallas kernels, project(): pl.pallas_call(functools.partial(project_kernel, sizes), out_shape=jax.Sh...  67.9 us
    pallas_call x1, Pallas kernels, send_back(): pl.pallas_call(functools.partial(return_kernel, (owners, chunks, width, b...  53.6 us
    pallas_call x1, Pallas kernels, recur(): pl.pallas_call(functools.partial(recur_kernel, tokens), out_shape=(jax.Sh...  29.3 us
    pallas_call x1, Pallas kernels, total(): pl.pallas_call(functools.partial(total_kernel, (lines, pieces, piece)), o...  15.5 us
    unnamed x1, blocking collectives  9.89 us
    pallas_call x1, Pallas kernels, mix(): pl.pallas_call(functools.partial(mix_kernel, tokens), grid=(channels // w...  6.14 us

profile of v4, /device:TPU:0, one launch (start us, length us, event | category | flops | bytes accessed | tf_op | source)
XLA Modules:
  0.0 199.8 jit_solution(484146546536384690)
XLA Ops:
  0.6 0.9 select_reduce_fusion.3
  1.6 1.2 dynamic-slice
  3.5 0.8 add_multiply_fusion
  4.3 9.9 %all-reduce = s32[256]{0:T(256)S(1)} all-reduce(s32[256]{0:T(256)S(1)} %get-tuple-element.21), channel_id=2, replica_groups=mesh['groups'=2,'tensor'=4,'dp'=4] {'dp'}, use_global_device_ids=true, to_apply=%add | all-reduce | flops 256 | bytes 2048
  14.1 0.1 reshape.232
  14.3 0.2 select_reduce_fusion
  14.5 0.1 broadcast_add_fusion
  14.6 0.1 add.172
  14.6 0.1 broadcast_in_dim.85
  14.7 0.1 select_n.70
  14.8 0.1 select_reduce_fusion.1
  14.9 0.0 copy-start
  15.0 0.8 select_n.78.slot_ref
  15.8 0.1 iota_add_fusion
  15.9 0.7 add.169.request_ref
  16.6 0.7 add.184.base_col_ref
  17.3 0.7 add.180.base_row_ref
  17.9 67.9 %shard_map.166.inputs_ref = bf16[320,2048]{1,0:T(8,128)(2,1)} custom-call(bf16[256,2048]{1,0:T(8,128)(2,1)} %hidden_ref.1, bf16[8192,2048]{1,0:T(8,128)(2,1)} %weight_ref.1, s32[1,256]{1,0:T(1,128)} %add.169.request_ref, s32[320,1]{1,0:T(8,128)} %select_n.78.slot_ref, s32[128,1]{1,0:T(8,128)} %add.184.base_col_ref, s32[1,128]{1,0:T(1,128)} %add.180.base_row_ref), custom_call_target="tpu_custom_call" | custom-call | flops 10737418240 | bytes 33554432 | tf_op jit(solution)/shard_map/pallas_call | solution.py:219
  85.8 0.0 copy-done
  85.9 0.7 copy.28.accepted_ref
  86.6 6.1 %shard_map.167 = (bf16[320,2048]{1,0:T(8,128)(2,1)}, f32[320,544]{1,0:T(8,128)}, bf16[3,80,2048]{2,1,0:T(8,128)(2,1)}) custom-call(bf16[320,2048]{1,0:T(8,128)(2,1)} %shard_map.166.inputs_ref, bf16[3,80,2048]{2,1,0:T(8,128)(2,1)} %bitcast.10, f32[4,2048]{1,0:T(4,128)} %taps_ref.1, f32[1,2048]{1,0:T(1,128)} %bitcast.11, bf16[544,2048]{1,0:T(8,128)(2,1)} %bitcast.9, ...), custom_call_target="tpu_custom_call" | custom-call | tf_op jit(solution)/shard_map/pallas_call | solution.py:381
  92.7 15.5 %shard_map.168.projected_ref = f32[320,544]{1,0:T(8,128)} custom-call(f32[320,544]{1,0:T(8,128)} %get-tuple-element.8.mine_ref), custom_call_target="tpu_custom_call" | custom-call | tf_op jit(solution)/shard_map/pallas_call | solution.py:485
  108.2 1.1 fusion.3
  109.3 2.0 broadcast_in_dim.100.outof_ref
  111.3 1.9 broadcast_in_dim.99.into_ref
  113.2 29.3 %shard_map.169 = (bf16[320,2048]{1,0:T(8,128)(2,1)}, bf16[80,16,2048]{2,1,0:T(8,128)(2,1)}) custom-call(s32[80]{0:T(128)} %copy-done, f32[320,544]{1,0:T(8,128)} %shard_map.168.projected_ref, f32[1,512]{1,0:T(1,128)} %bitcast.15, bf16[512,2048]{1,0:T(8,128)(2,1)} %step_weight_ref.1, f32[1,2048]{1,0:T(1,128)} %bitcast.12, f32[16,2048]{1,0:T(8,128)} %decay_ref.1, ...), custom_call_target="tpu_custom_call" | custom-call | tf_op jit(solution)/shard_map/pallas_call | solution.py:602
  142.5 0.7 select_n.77.slot_ref
  143.1 0.7 add.185.request_ref
  143.9 53.6 %shard_map.170 = bf16[256,2048]{1,0:T(8,128)(2,1)} custom-call(bf16[320,2048]{1,0:T(8,128)(2,1)} %get-tuple-element.10.rows_ref, s32[256,1]{1,0:T(8,128)} %add.185.request_ref, s32[1,320]{1,0:T(1,128)} %select_n.77.slot_ref, s32[128,1]{1,0:T(8,128)} %add.184.base_col_ref, s32[1,128]{1,0:T(1,128)} %add.180.base_row_ref), custom_call_target="tpu_custom_call" | custom-call | tf_op jit(solution)/shard_map/pallas_call | solution.py:311
  197.5 2.3 %copy.33 = bf16[256,2048]{1,0:T(8,128)(2,1)} copy(bf16[256,2048]{1,0:T(8,128)(2,1)} %shard_map.170) | data formatting | bytes 2097152
  (9 shorter events, 0.1 us)
Async XLA Ops:
  14.9 70.9 %copy-start = (s32[80]{0:T(128)}, s32[80]{0:T(128)S(1)}, u32[]{:S(2)}) copy-start(s32[80]{0:T(128)S(1)} %get-tuple-element.14.accepted_ref) | copy-start | bytes 964
